TPU v7x, 128 devices: a whole 4x4x4 slice. The times are simulated.
128 devices in a mesh: dp: 32 (over x, z, core), mp: 4 (over y).
Axes of the slice: x: 4, y: 4, z: 4, core: 2. Of those that a mesh axis runs over, the one named last changes fastest.
Arguments:
- states: bfloat16 [8192, 2048], P('dp'), may hold values from -6 to 6
- w_query: bfloat16 [2048, 2048], P(None, 'mp'), may hold values from -0.125 to 0.125
- w_key: bfloat16 [2048, 2048], P(None, 'mp'), may hold values from -0.125 to 0.125
- w_value: bfloat16 [2048, 2048], P(None, 'mp'), may hold values from -0.125 to 0.125
- w_out: bfloat16 [2048, 2048], P('mp'), may hold values from -0.125 to 0.125
- w_gate: bfloat16 [2048, 8192], P(None, 'mp'), may hold values from -0.125 to 0.125
- w_up: bfloat16 [2048, 8192], P(None, 'mp'), may hold values from -0.125 to 0.125
- w_down: bfloat16 [8192, 2048], P('mp'), may hold values from -0.0625 to 0.0625
- q_gain: float32 [2048], P('mp'), may hold values from 0.1 to 1.9
- k_gain: float32 [2048], P('mp'), may hold values from 0.1 to 1.9
- attn_gain: float32 [2048], replicated, may hold values from 0.1 to 1.9
- mlp_gain: float32 [2048], replicated, may hold values from 0.1 to 1.9
- cotangent: bfloat16 [8192, 2048], P('dp'), may hold values from -6 to 6
- segments: int32 [8192], replicated, may hold values from 0 to 13, as said below
- sources: int32 [8192], P('dp'), may hold values from 0 to 7
- group_weights: int32 [8], replicated, may hold values from 4 to 32
Outputs:
- output: bfloat16 [8192, 2048], P('dp')
- grad_states: float32 [8192, 2048], P('dp')
- grad_query: float32 [2048, 2048], P('dp', 'mp')
- grad_key: float32 [2048, 2048], P('dp', 'mp')
- grad_value: float32 [2048, 2048], P('dp', 'mp')
- grad_out: float32 [2048, 2048], P('mp', 'dp')
- grad_gate: float32 [2048, 8192], P('dp', 'mp')
- grad_up: float32 [2048, 8192], P('dp', 'mp')
- grad_down: float32 [8192, 2048], P('mp', 'dp')
- grad_q_gain: float32 [2048], P('mp')
- grad_k_gain: float32 [2048], P('mp')
- grad_attn_gain: float32 [2048], replicated
- grad_mlp_gain: float32 [2048], replicated
Inputs may be any that keep to these rules, and one draw needn't show every extreme that they name: `segments`: document ids never fall along the tokens; a new document begins at every multiple of 4096; a sequence holds at most seven documents; in each sequence one document runs from its first 256 tokens into its last 256.
All inputs are finite; a program needn't handle non-finite values.
Results may differ from a plain program's by a relative error of at most 0.035.
Values may be sent and summed in bfloat16 or wider, within the bound.
No kernel may reach another device: no remote copies, remote signals or barrier semaphores. Data moves between devices by JAX's collectives and lax.ppermute only.
A program may use at most 320 MiB of HBM per device.

v0:
```python
import jax
import jax.numpy as jnp
from jax import lax
from jax.sharding import PartitionSpec as P

HD = 128
SEQ_MAX = 4096


epsilon = 1e-06
theta_base = 500000.0
weight_unit = 16.0
far_below = -1e30


def product(left, right):
    return jnp.dot(left, right, preferred_element_type=jnp.float32)


def product_left(left, right):
    return lax.dot_general(
        left, right, (((0,), (0,)), ((), ())), preferred_element_type=jnp.float32
    )


def product_right(left, right):
    return lax.dot_general(
        left, right, (((1,), (1,)), ((), ())), preferred_element_type=jnp.float32
    )


def tables(positions, head_width):
    inverse = 1.0 / theta_base ** (jnp.arange(0, head_width, 2, dtype=jnp.float32) / head_width)
    angles = positions.astype(jnp.float32)[:, None] * inverse[None, :]
    angles = jnp.concatenate([angles, angles], axis=-1)
    return (jnp.cos(angles), jnp.sin(angles))


def rotate(values, cosine_table, sine_table, direction):
    half_width = values.shape[-1] // 2
    turned = jnp.concatenate([-values[..., half_width:], values[..., :half_width]], axis=-1)
    return values * cosine_table[:, None, :] + direction * turned * sine_table[:, None, :]


def allowed_mask(row_pos, row_seg, col_pos, col_seg, seq_len):
    same_sequence = row_pos[:, None] // seq_len == col_pos[None, :] // seq_len
    return (
        same_sequence
        & (row_seg[:, None] == col_seg[None, :])
        & (row_pos[:, None] >= col_pos[None, :])
    )


def local(
    states,
    w_query,
    w_key,
    w_value,
    w_out,
    w_gate,
    w_up,
    w_down,
    q_gain,
    k_gain,
    attn_gain,
    mlp_gain,
    cotangent,
    segments,
    sources,
    group_weights,
):
    tokens = states.shape[0]
    model_width = states.shape[1]
    local_heads = w_query.shape[1] // HD
    score_scale = HD ** (-0.5)
    total_tokens = tokens * lax.axis_size("dp")
    seq_len = min(SEQ_MAX, total_tokens)
    first_pos = lax.axis_index("dp") * tokens
    seq_start = first_pos // seq_len * seq_len
    q_pos = first_pos + jnp.arange(tokens, dtype=jnp.int32)
    q_seg = lax.dynamic_slice_in_dim(segments, first_pos, tokens)
    last_pos = first_pos + tokens - 1
    cosine_table, sine_table = tables(q_pos % seq_len, HD)
    query_raw = product(states, w_query)
    key_raw = product(states, w_key)
    value_low = product(states, w_value).astype(jnp.bfloat16)
    q_square, k_square = lax.psum(
        (jnp.sum(query_raw * query_raw, axis=1), jnp.sum(key_raw * key_raw, axis=1)), "mp"
    )
    q_rate = lax.rsqrt(q_square / model_width + epsilon)
    k_rate = lax.rsqrt(k_square / model_width + epsilon)
    q_norm = (query_raw * q_rate[:, None] * q_gain).reshape(tokens, local_heads, HD)
    k_norm = (key_raw * k_rate[:, None] * k_gain).reshape(tokens, local_heads, HD)
    q_rot = rotate(q_norm, cosine_table, sine_table, 1.0).astype(jnp.bfloat16)
    k_rot = rotate(k_norm, cosine_table, sine_table, 1.0).astype(jnp.bfloat16)
    value_heads = value_low.reshape(tokens, local_heads, HD)
    start_state = (
        jnp.full((local_heads, tokens), far_below, jnp.float32),
        jnp.zeros((local_heads, tokens), jnp.float32),
        jnp.zeros((local_heads, tokens, HD), jnp.float32),
    )
    offset = jnp.int32(0)
    key_piece = lax.all_gather(k_rot, "dp", axis=0, tiled=True)
    value_piece = lax.all_gather(value_heads, "dp", axis=0, tiled=True)
    row_count = key_piece.shape[0]
    col_pos = jnp.arange(row_count, dtype=jnp.int32)
    col_seg = segments
    allowed = allowed_mask(q_pos, q_seg, col_pos, col_seg, seq_len)

    def forward_compute(state_now):
        row_top, row_total, weighted = state_now
        scores = (
            jnp.einsum("qhd,khd->hqk", q_rot, key_piece, preferred_element_type=jnp.float32)
            * score_scale
        )
        scores = jnp.where(allowed[None], scores, far_below)
        new_top = jnp.maximum(row_top, jnp.max(scores, axis=-1))
        weights = jnp.exp(scores - new_top[..., None])
        row_total = jnp.sum(weights, axis=-1)
        weighted = jnp.einsum(
            "hqk,khd->hqd",
            weights.astype(jnp.bfloat16),
            value_piece,
            preferred_element_type=jnp.float32,
        )
        return (new_top, row_total, weighted)

    active = (offset <= last_pos) & (offset + row_count - 1 >= seq_start)
    row_top, row_total, weighted = lax.cond(
        active, forward_compute, lambda unchanged: unchanged, start_state
    )
    log_total = row_top + jnp.log(row_total)
    mixed_full = jnp.transpose(weighted / row_total[..., None], (1, 0, 2))
    mixed_low = mixed_full.reshape(tokens, -1).astype(jnp.bfloat16)
    branch = lax.psum(product(mixed_low, w_out).astype(jnp.bfloat16), "mp").astype(jnp.float32)
    b_rate = lax.rsqrt(jnp.mean(branch * branch, axis=1, keepdims=True) + epsilon)
    b_norm = branch * b_rate
    hidden = states.astype(jnp.float32) + attn_gain * b_norm
    hidden_low = hidden.astype(jnp.bfloat16)
    gate_proj = product(hidden_low, w_gate)
    up_proj = product(hidden_low, w_up)
    sigmoid_gate = jax.nn.sigmoid(gate_proj)
    silu_gate = gate_proj * sigmoid_gate
    act_low = (silu_gate * up_proj).astype(jnp.bfloat16)
    down_proj = lax.psum(product(act_low, w_down).astype(jnp.bfloat16), "mp").astype(jnp.float32)
    d_rate = lax.rsqrt(jnp.mean(down_proj * down_proj, axis=1, keepdims=True) + epsilon)
    d_norm = down_proj * d_rate
    output = (hidden + mlp_gain * d_norm).astype(jnp.bfloat16)
    chosen = sources[:, None] == jnp.arange(group_weights.shape[0], dtype=jnp.int32)[None, :]
    token_share = (
        jnp.sum(jnp.where(chosen, group_weights[None, :], 0), axis=1).astype(jnp.float32)
        / weight_unit
    )
    grad_top = cotangent.astype(jnp.float32) * token_share[:, None]
    local_mlp_gain = jnp.sum(grad_top * d_norm, axis=0)
    scaled_top = mlp_gain * grad_top
    grad_down_proj = (
        d_rate * (scaled_top - d_norm * jnp.mean(scaled_top * d_norm, axis=1, keepdims=True))
    ).astype(jnp.bfloat16)
    grad_act = product_right(grad_down_proj, w_down)
    grad_gate_proj = (
        grad_act * up_proj * sigmoid_gate * (1.0 + gate_proj * (1.0 - sigmoid_gate))
    ).astype(jnp.bfloat16)
    grad_up_proj = (grad_act * silu_gate).astype(jnp.bfloat16)
    hidden_part = product_right(grad_gate_proj, w_gate) + product_right(grad_up_proj, w_up)
    grad_hidden = grad_top + lax.psum(hidden_part.astype(jnp.bfloat16), "mp").astype(jnp.float32)
    local_attn_gain = jnp.sum(grad_hidden * b_norm, axis=0)
    scaled_hidden = attn_gain * grad_hidden
    grad_branch = (
        b_rate * (scaled_hidden - b_norm * jnp.mean(scaled_hidden * b_norm, axis=1, keepdims=True))
    ).astype(jnp.bfloat16)
    grad_mixed = product_right(grad_branch, w_out).astype(jnp.bfloat16)
    grad_mixed_heads = grad_mixed.reshape(tokens, local_heads, HD)
    row_delta = jnp.transpose(jnp.sum(grad_mixed_heads.astype(jnp.float32) * mixed_full, axis=-1))
    every_key = jnp.zeros((total_tokens, local_heads, HD), jnp.float32)
    back_start = (jnp.zeros((tokens, local_heads, HD), jnp.float32), every_key, every_key)
    offset = jnp.int32(0)
    backward_key_piece = lax.all_gather(k_rot, "dp", axis=0, tiled=True)
    backward_value_piece = lax.all_gather(value_heads, "dp", axis=0, tiled=True)
    row_count = backward_key_piece.shape[0]
    col_pos = jnp.arange(row_count, dtype=jnp.int32)
    col_seg = segments
    backward_allowed = allowed_mask(q_pos, q_seg, col_pos, col_seg, seq_len)

    def backward_compute(state_now):
        scores = (
            jnp.einsum(
                "qhd,khd->hqk", q_rot, backward_key_piece, preferred_element_type=jnp.float32
            )
            * score_scale
        )
        scores = jnp.where(backward_allowed[None], scores, far_below)
        probs = jnp.exp(scores - log_total[..., None])
        grad_probs = jnp.einsum(
            "qhd,khd->hqk",
            grad_mixed_heads,
            backward_value_piece,
            preferred_element_type=jnp.float32,
        )
        grad_scores = (probs * (grad_probs - row_delta[..., None])).astype(jnp.bfloat16)
        grad_now = (
            jnp.einsum(
                "hqk,khd->qhd", grad_scores, backward_key_piece, preferred_element_type=jnp.float32
            )
            * score_scale
        )
        key_part = (
            jnp.einsum("hqk,qhd->khd", grad_scores, q_rot, preferred_element_type=jnp.float32)
            * score_scale
        )
        value_part = jnp.einsum(
            "hqk,qhd->khd",
            probs.astype(jnp.bfloat16),
            grad_mixed_heads,
            preferred_element_type=jnp.float32,
        )
        return (grad_now, key_part, value_part)

    active = (offset <= last_pos) & (offset + row_count - 1 >= seq_start)
    grad_q_rot, key_total, value_total = lax.cond(
        active, backward_compute, lambda unchanged: unchanged, back_start
    )
    grad_k_rot, grad_value_raw = (
        lax.psum_scatter(
            key_total.astype(jnp.bfloat16), "dp", scatter_dimension=0, tiled=True
        ).astype(jnp.float32),
        lax.psum_scatter(
            value_total.astype(jnp.bfloat16), "dp", scatter_dimension=0, tiled=True
        ).astype(jnp.float32),
    )
    grad_q_norm = rotate(grad_q_rot, cosine_table, sine_table, -1.0).reshape(tokens, -1)
    grad_k_norm = rotate(grad_k_rot, cosine_table, sine_table, -1.0).reshape(tokens, -1)
    local_q_gain = jnp.sum(grad_q_norm * query_raw * q_rate[:, None], axis=0)
    local_k_gain = jnp.sum(grad_k_norm * key_raw * k_rate[:, None], axis=0)
    q_scaled = grad_q_norm * q_gain
    k_scaled = grad_k_norm * k_gain
    q_inner, k_inner = lax.psum(
        (jnp.sum(query_raw * q_scaled, axis=1), jnp.sum(key_raw * k_scaled, axis=1)), "mp"
    )
    grad_query_raw = (
        q_rate[:, None] * q_scaled
        - query_raw * (q_rate * q_rate * q_rate * q_inner / model_width)[:, None]
    ).astype(jnp.bfloat16)
    grad_key_raw = (
        k_rate[:, None] * k_scaled
        - key_raw * (k_rate * k_rate * k_rate * k_inner / model_width)[:, None]
    ).astype(jnp.bfloat16)
    grad_value_low = grad_value_raw.reshape(tokens, -1).astype(jnp.bfloat16)
    input_part = (
        product_right(grad_query_raw, w_query)
        + product_right(grad_key_raw, w_key)
        + product_right(grad_value_low, w_value)
    )
    grad_states = grad_hidden + lax.psum(input_part.astype(jnp.bfloat16), "mp").astype(jnp.float32)
    summed = (
        lax.psum_scatter(
            product_left(states, grad_query_raw).astype(jnp.bfloat16),
            "dp",
            scatter_dimension=0,
            tiled=True,
        ).astype(jnp.float32),
        lax.psum_scatter(
            product_left(states, grad_key_raw).astype(jnp.bfloat16),
            "dp",
            scatter_dimension=0,
            tiled=True,
        ).astype(jnp.float32),
        lax.psum_scatter(
            product_left(states, grad_value_low).astype(jnp.bfloat16),
            "dp",
            scatter_dimension=0,
            tiled=True,
        ).astype(jnp.float32),
        lax.psum_scatter(
            product_left(grad_branch, mixed_low).astype(jnp.bfloat16),
            "dp",
            scatter_dimension=0,
            tiled=True,
        ).astype(jnp.float32),
        lax.psum_scatter(
            product_left(hidden_low, grad_gate_proj).astype(jnp.bfloat16),
            "dp",
            scatter_dimension=0,
            tiled=True,
        ).astype(jnp.float32),
        lax.psum_scatter(
            product_left(hidden_low, grad_up_proj).astype(jnp.bfloat16),
            "dp",
            scatter_dimension=0,
            tiled=True,
        ).astype(jnp.float32),
        lax.psum_scatter(
            product_left(grad_down_proj, act_low).astype(jnp.bfloat16),
            "dp",
            scatter_dimension=0,
            tiled=True,
        ).astype(jnp.float32),
    )
    grad_q_gain, grad_k_gain, grad_attn_gain, grad_mlp_gain = lax.psum(
        (local_q_gain, local_k_gain, local_attn_gain, local_mlp_gain), "dp"
    )
    return (
        output,
        grad_states,
        summed[0],
        summed[1],
        summed[2],
        jnp.transpose(summed[3]),
        summed[4],
        summed[5],
        jnp.transpose(summed[6]),
        grad_q_gain,
        grad_k_gain,
        grad_attn_gain,
        grad_mlp_gain,
    )


def solution(mesh):
    placed = (
        P("dp", None),
        P(None, "mp"),
        P(None, "mp"),
        P(None, "mp"),
        P("mp", None),
        P(None, "mp"),
        P(None, "mp"),
        P("mp", None),
        P("mp"),
        P("mp"),
        P(),
        P(),
        P("dp", None),
        P(),
        P("dp"),
        P(),
    )
    return jax.shard_map(
        local,
        mesh=mesh,
        in_specs=placed,
        out_specs=(
            P("dp", None),
            P("dp", None),
            P("dp", "mp"),
            P("dp", "mp"),
            P("dp", "mp"),
            P("mp", "dp"),
            P("dp", "mp"),
            P("dp", "mp"),
            P("mp", "dp"),
            P("mp"),
            P("mp"),
            P(),
            P(),
        ),
        check_vma=False,
    )
```

profile of v0, /device:TPU:0, one launch (start us, length us, event | category | flops | bytes accessed | tf_op | source)
XLA Modules:
  0.0 1322.2 jit_solution(1129527522846701560)
XLA Ops:
  7.3 2.8 fusion.55
  10.9 1.5 multiply_reduce_fusion.3
  14.0 10.8 all-reduce.2
  31.0 3.4 fusion.23
  34.4 32.1 %all-gather.5.cloned.1.call-done = bf16[8192,4,128]{2,0,1:T(8,128)(2,1)} async-done(((bf16[256,4,128]{2,0,1:T(8,128)(2,1)}), bf16[8192,4,128]{2,0,1:T(8,128)(2,1)}) %all-gather.5.cloned.1.call-update) | async-done | bytes 8388624 | tf_op jit(solution)/shard_map/all_gather | solution.py:104
  66.5 55.5 %all-gather.3.cloned.1.call-done = bf16[8192,4,128]{2,0,1:T(8,128)(2,1)} async-done(((bf16[256,4,128]{2,0,1:T(8,128)(2,1)}), bf16[8192,4,128]{2,0,1:T(8,128)(2,1)}) %all-gather.3.cloned.1.call-update) | async-done | bytes 8388624 | tf_op jit(solution)/shard_map/all_gather | solution.py:103
  122.1 51.9 %conditional.2 = (f32[4,256]{1,0:T(4,128)}, f32[4,256]{1,0:T(4,128)}, f32[4,256]{1,0:T(4,128)S(1)}, f32[4,256,128]{1,2,0:T(8,128)}) conditional(s32[]{:T(128)} %convert_element_type.167, () %tuple.26, (pred[256,8192]{1,0:T(8,128)(4,1)}, bf16[256,4,128]{2,0,1:T(8,128)(2,1)S(1)}, bf16[8192,4,128]{2,0,1:T(8,128)(2,1)}, ...), branch_computations={%region_4.5_spmd, %region_5.8_spmd} | conditional | flops 4387240960 | bytes 124551200 | solution.py:129
  122.6 16.5 %fusion = (f32[4,256]{1,0:T(4,128)S(1)}, f32[4,256,8192]{2,1,0:T(8,128)}) fusion(pred[256,8192]{1,0:T(8,128)(4,1)} %get-tuple-element.26, bf16[256,4,128]{2,0,1:T(8,128)(2,1)S(1)} %get-tuple-element.27, bf16[8192,4,128]{2,0,1:T(8,128)(2,1)} %get-tuple-element.28), kind=kOutput, calls=%fused_computation.2 | convolution fusion | flops 2172648448 | bytes 44306432 | tf_op jit(solution)/shard_map/cond/branch_1_fun/qhd,khd->hqk/dot_general | solution.py:113
  139.7 17.8 %fusion.3 = f32[4,256,128]{1,2,0:T(8,128)} fusion(bf16[8192,4,128]{2,0,1:T(8,128)(2,1)} %get-tuple-element.29, f32[4,256,8192]{2,1,0:T(8,128)} %get-tuple-element.167, f32[4,256]{1,0:T(4,128)} %broadcast_maximum_fusion, pred[256,8192]{1,0:T(8,128)(4,1)} %get-tuple-element.26), kind=kOutput, calls=%fused_computation.5 | convolution fusion | flops 2181038080 | bytes 44568576 | tf_op jit(solution)/shard_map/cond | solution.py:129
  157.5 15.8 %fusion.2 = f32[4,256]{1,0:T(4,128)} fusion(f32[4,256,8192]{2,1,0:T(8,128)} %get-tuple-element.167, f32[4,256]{1,0:T(4,128)} %broadcast_maximum_fusion, pred[256,8192]{1,0:T(8,128)(4,1)} %get-tuple-element.26), kind=kLoop, calls=%fused_computation.4 | loop fusion | flops 33553408 | bytes 35659776 | tf_op jit(solution)/shard_map/cond/branch_1_fun/reduce_sum | solution.py:119
  175.8 3.3 convolution_convert_fusion.7
  179.3 45.3 %all-reduce.8.cloned.1.call-done = bf16[256,2048]{1,0:T(8,128)(2,1)} async-done(((bf16[256,2048]{1,0:T(8,128)(2,1)}), bf16[256,2048]{1,0:T(8,128)(2,1)}) %all-reduce.8.cloned.1.call-update) | async-done | bytes 1048592 | tf_op jit(solution)/shard_map/psum | solution.py:135
  224.6 1.5 fusion.43
  226.1 1.9 fusion.54
  228.1 6.1 fusion.84
  234.3 3.9 multiply_convert_fusion.3
  239.2 3.3 convolution_convert_fusion.8
  243.1 46.2 %all-reduce.10.cloned.1.call-done = bf16[256,2048]{1,0:T(8,128)(2,1)} async-done(((bf16[256,2048]{1,0:T(8,128)(2,1)}), bf16[256,2048]{1,0:T(8,128)(2,1)}) %all-reduce.10.cloned.1.call-update) | async-done | bytes 1048592 | tf_op jit(solution)/shard_map/psum | solution.py:145
  289.3 1.7 fusion.51
  291.0 2.3 fusion.50
  293.3 7.8 multiply_convert_fusion.1
  301.1 2.4 fusion.85
  303.5 6.8 fusion.35
  310.3 46.7 %all-reduce.12.cloned.1.call-done = bf16[256,2048]{1,0:T(8,128)(2,1)} async-done(((bf16[256,2048]{1,0:T(8,128)(2,1)}), bf16[256,2048]{1,0:T(8,128)(2,1)}) %all-reduce.12.cloned.1.call-update) | async-done | bytes 1048592 | tf_op jit(solution)/shard_map/psum | solution.py:166
  357.1 2.7 fusion.42
  359.8 3.7 fusion.41
  366.0 1.7 reshape.245
  367.7 1.8 copy.91
  370.8 87.8 %conditional.3 = (f32[256,4,128]{2,0,1:T(8,128)}, bf16[8192,4,128]{2,0,1:T(8,128)(2,1)}, bf16[8192,4,128]{2,0,1:T(8,128)(2,1)}) conditional(s32[]{:T(128)} %convert_element_type.167, () %tuple.28, (pred[256,8192]{1,0:T(8,128)(4,1)}, bf16[256,4,128]{2,0,1:T(8,128)(2,1)S(1)}, bf16[8192,4,128]{2,0,1:T(8,128)(2,1)}, f32[4,256]{1,0:T(4,128)}, ...), branch_computations={%region_17.18_spmd, %region_18.19_spmd} | conditional | flops 10829825024 | bytes 198729760 | solution.py:220
  371.6 16.5 %fusion.83 = f32[4,256,8192]{2,1,0:T(8,128)} fusion(bf16[256,4,128]{2,0,1:T(8,128)(2,1)S(1)} %get-tuple-element.31, bf16[8192,4,128]{2,0,1:T(8,128)(2,1)} %get-tuple-element.32), kind=kOutput, calls=%fused_computation.164 | convolution fusion | flops 2147483648 | bytes 42205184 | tf_op jit(solution)/shard_map/cond/branch_1_fun/qhd,khd->hqk/dot_general | solution.py:187
  388.1 24.8 %multiply_convert_fusion = bf16[4,256,8192]{2,1,0:T(8,128)(2,1)} fusion(f32[4,256,8192]{2,1,0:T(8,128)} %fusion.83, bf16[8192,4,128]{2,0,1:T(8,128)(2,1)} %get-tuple-element.36, f32[4,256]{1,0:T(4,128)S(1)} %get-tuple-element.37, f32[4,256]{1,0:T(4,128)S(1)} %add.131, pred[256,8192]{1,0:T(8,128)(4,1)} %get-tuple-element.30, ...), kind=kOutput, calls=%fused_computation.10 | convolution fusion | flops 2197815296 | bytes 61087744 | tf_op jit(solution)/shard_map/cond/branch_1_fun/qhd,khd->hqk/dot_general | solution.py:194
  413.0 19.6 %fusion.15 = bf16[8192,4,128]{2,0,1:T(8,128)(2,1)} fusion(f32[4,256,8192]{2,1,0:T(8,128)} %fusion.83, f32[4,256]{1,0:T(4,128)S(1)} %add.131, pred[256,8192]{1,0:T(8,128)(4,1)} %get-tuple-element.30, bf16[256,4,128]{2,1,0:T(4,128)(2,1)} %get-tuple-element.133), kind=kOutput, calls=%fused_computation.19 | convolution fusion | flops 2181038080 | bytes 44306432 | tf_op jit(solution)/shard_map/cond/branch_1_fun/hqk,qhd->khd/dot_general | solution.py:211
  432.6 13.5 %fusion.18 = f32[256,4,128]{2,0,1:T(8,128)} fusion(bf16[4,256,8192]{2,1,0:T(8,128)(2,1)} %multiply_convert_fusion, bf16[8192,4,128]{2,0,1:T(8,128)(2,1)} %get-tuple-element.32), kind=kOutput, calls=%fused_computation.21 | convolution fusion | flops 2147614720 | bytes 25690112 | tf_op jit(solution)/shard_map/cond/branch_1_fun/hqk,khd->qhd/dot_general | solution.py:202
  446.0 12.1 multiply_bitcast_fusion
  458.6 12.1 copy.95
  471.6 3.4 convolution_convert_fusion.3
  475.1 7.3 convolution_convert_fusion.1
  482.5 7.3 convolution_convert_fusion.2
  489.8 7.7 convolution_convert_fusion
  497.6 2.4 slice_negate_fusion.3
  500.1 52.3 %reduce-scatter.16.cloned.1.call-done = bf16[256,4,128]{2,0,1:T(8,128)(2,1)} async-done(((bf16[8192,4,128]{2,0,1:T(8,128)(2,1)}), bf16[256,4,128]{2,0,1:T(8,128)(2,1)}) %reduce-scatter.16.cloned.1.call-update) | async-done | bytes 262160 | tf_op jit(solution)/shard_map/reduce_scatter | solution.py:224
  557.2 10.4 all-reduce.1
  572.2 2.1 convolution_add_fusion.1
  574.3 73.8 %reduce-scatter.18.cloned.1.call-done = bf16[256,4,128]{0,2,1:T(8,128)(2,1)} async-done(((bf16[8192,4,128]{0,2,1:T(8,128)(2,1)}), bf16[256,4,128]{0,2,1:T(8,128)(2,1)}) %reduce-scatter.18.cloned.1.call-update) | async-done | bytes 262160 | tf_op jit(solution)/shard_map/reduce_scatter | solution.py:227
  648.1 4.1 fusion.36
  652.4 3.4 fusion.25
  655.8 3.9 copy.103
  659.8 3.3 fusion.24
  663.1 4.0 copy.101
  668.0 3.3 fusion.26
  671.3 4.0 copy.105
  675.3 55.0 %reduce-scatter.20.cloned.1.call-done = bf16[64,512]{1,0:T(8,128)(2,1)} async-done(((bf16[2048,512]{1,0:T(8,128)(2,1)}), bf16[64,512]{1,0:T(8,128)(2,1)}) %reduce-scatter.20.cloned.1.call-update) | async-done | bytes 65552 | tf_op jit(solution)/shard_map/reduce_scatter | solution.py:274
  730.3 1.5 convert_bitcast_fusion.1
  731.8 94.7 %reduce-scatter.24.cloned.1.call-done = bf16[64,2048]{1,0:T(8,128)(2,1)} async-done(((bf16[2048,2048]{1,0:T(8,128)(2,1)}), bf16[64,2048]{1,0:T(8,128)(2,1)}) %reduce-scatter.24.cloned.1.call-update) | async-done | bytes 262160 | tf_op jit(solution)/shard_map/reduce_scatter | solution.py:286
  826.5 1.8 convert_element_type.212
  828.3 93.9 %reduce-scatter.22.cloned.1.call-done = bf16[64,2048]{1,0:T(8,128)(2,1)} async-done(((bf16[2048,2048]{1,0:T(8,128)(2,1)}), bf16[64,2048]{1,0:T(8,128)(2,1)}) %reduce-scatter.22.cloned.1.call-update) | async-done | bytes 262160 | tf_op jit(solution)/shard_map/reduce_scatter | solution.py:280
  922.2 1.8 convert_element_type.210
  924.0 94.5 %reduce-scatter.26.cloned.1.call-done = bf16[64,2048]{1,0:T(8,128)(2,1)} async-done(((bf16[2048,2048]{1,0:T(8,128)(2,1)}), bf16[64,2048]{1,0:T(8,128)(2,1)}) %reduce-scatter.26.cloned.1.call-update) | async-done | bytes 262160 | tf_op jit(solution)/shard_map/reduce_scatter | solution.py:292
  1018.4 1.8 convert_bitcast_fusion
  1020.2 124.5 %all-reduce = (f32[512]{0:T(512)}, f32[512]{0:T(512)}, f32[2048]{0:T(1024)}, f32[2048]{0:T(1024)}) all-reduce(f32[512]{0:T(512)S(1)} %get-tuple-element.156, f32[512]{0:T(512)S(1)} %get-tuple-element.154, f32[2048]{0:T(1024)S(1)} %get-tuple-element.150, f32[2048]{0:T(1024)S(1)} %get-tuple-element.152), channel_id=1, replica_groups=mesh['dp'=32,'mp'=4] {'dp'}, use_global_device_ids=true, to_apply=%region_34.35 | all-reduce | flops 5120 | bytes 40960 | tf_op jit(solution)/shard_map/psum | solution.py:299
  1144.7 3.5 convert_add_fusion
  1148.2 1.5 reduce-scatter.30.cloned.1.call-done
  1151.4 80.4 %reduce-scatter.28.cloned.1.call-done = bf16[64,512]{1,0:T(8,128)(2,1)} async-done(((bf16[2048,512]{1,0:T(8,128)(2,1)}), bf16[64,512]{1,0:T(8,128)(2,1)}) %reduce-scatter.28.cloned.1.call-update) | async-done | bytes 65552
  1233.5 80.3 %reduce-scatter.32.cloned.1.call-done = bf16[64,512]{1,0:T(8,128)(2,1)} async-done(((bf16[2048,512]{1,0:T(8,128)(2,1)}), bf16[64,512]{1,0:T(8,128)(2,1)}) %reduce-scatter.32.cloned.1.call-update) | async-done | bytes 65552
  (188 shorter events, 34.8 us)
Async XLA Ops:
  7.2 3.7 copy-start
  7.2 3.7 copy-start.2
  7.2 59.3 %all-gather.5.cloned.1.call-start = ((), (), s32[]{:S(2)}) async-start(), calls=%async_computation.10 | async-start | bytes 8650752 | tf_op jit(solution)/shard_map/all_gather | solution.py:104
  10.8 111.3 %all-gather.3.cloned.1.call-start = ((), (), s32[]{:S(2)}) async-start(), calls=%async_computation.9 | async-start | bytes 8650752 | tf_op jit(solution)/shard_map/all_gather | solution.py:103
  10.9 1.6 copy-start.19
  12.5 13.7 %copy-start.36 = (f32[512]{0:T(512)S(1)}, f32[512]{0:T(512)}, u32[]{:S(2)}) copy-start(f32[512]{0:T(512)} %param.29) | copy-start | bytes 6148
  12.5 14.9 %copy-start.34 = (f32[512]{0:T(512)S(1)}, f32[512]{0:T(512)}, u32[]{:S(2)}) copy-start(f32[512]{0:T(512)} %param.28) | copy-start | bytes 6148
  24.8 4.0 copy-start.42
  24.8 4.0 copy-start.44
  26.1 2.9 copy-start.24
  26.1 2.9 copy-start.38
  26.1 2.9 copy-start.40
  28.5 1.0 copy-start.8
  28.5 1.2 copy-start.10
  29.7 1.2 copy-start.33
  30.9 193.7 %all-reduce.8.cloned.1.call-start = ((), (), s32[]{:S(2)}) async-start(), calls=%async_computation.11 | async-start | bytes 2097152 | tf_op jit(solution)/shard_map/psum | solution.py:135
  175.8 50.3 %copy-start.32 = (f32[2048]{0:T(1024)S(1)}, f32[2048]{0:T(1024)}, u32[]{:S(2)}) copy-start(f32[2048]{0:T(1024)} %param.30) | copy-start | bytes 24580
  179.1 110.2 %all-reduce.10.cloned.1.call-start = ((), (), s32[]{:S(2)}) async-start(), calls=%async_computation.12 | async-start | bytes 2097152 | tf_op jit(solution)/shard_map/psum | solution.py:145
  226.1 8.1 slice-start.4
  228.1 6.2 copy-start.7
  228.1 6.2 slice-start.5
  228.1 11.0 slice-start
  234.3 3.9 copy-start.48
  234.3 4.9 slice-start.1
  238.2 1.0 copy-start.26
  239.2 3.8 copy-start.46
  239.2 3.8 copy-start.47
  242.5 48.5 %copy-start.1 = (bf16[256,2048]{1,0:T(8,128)(2,1)S(1)}, bf16[256,2048]{1,0:T(8,128)(2,1)}, u32[]{:S(2)}) copy-start(bf16[256,2048]{1,0:T(8,128)(2,1)} %param.32) | copy-start | bytes 3145732
  242.5 48.5 %copy-start.31 = (f32[2048]{0:T(1024)S(1)}, f32[2048]{0:T(1024)}, u32[]{:S(2)}) copy-start(f32[2048]{0:T(1024)} %param.31) | copy-start | bytes 24580
  242.5 114.5 %all-reduce.12.cloned.1.call-start = ((), (), s32[]{:S(2)}) async-start(), calls=%async_computation.13 | async-start | bytes 2097152 | tf_op jit(solution)/shard_map/psum | solution.py:166
  289.3 4.0 copy-start.4
  289.3 11.8 slice-start.2
  293.3 7.8 slice-start.3
  301.0 2.4 copy-start.27
  301.1 2.4 copy-start.28
  310.3 242.0 %reduce-scatter.16.cloned.1.call-start = ((), (), s32[]{:S(2)}) async-start(), calls=%async_computation.14 | async-start | bytes 8650752 | tf_op jit(solution)/shard_map/reduce_scatter | solution.py:224
  357.1 2.7 copy-start.3
  357.1 2.7 copy-start.5
  357.1 2.7 copy-start.6
  359.8 4.7 copy-start.21
  363.5 1.0 copy-start.14
  458.6 189.5 %reduce-scatter.18.cloned.1.call-start = ((), (), s32[]{:S(2)}) async-start(), calls=%async_computation.15 | async-start | bytes 8650752 | tf_op jit(solution)/shard_map/reduce_scatter | solution.py:227
  470.7 259.6 %reduce-scatter.20.cloned.1.call-start = ((), (), s32[]{:S(2)}) async-start(), calls=%async_computation.17 | async-start | bytes 2162688 | tf_op jit(solution)/shard_map/reduce_scatter | solution.py:274
  475.0 351.5 %reduce-scatter.24.cloned.1.call-start = ((), (), s32[]{:S(2)}) async-start(), calls=%async_computation.19 | async-start | bytes 8650752 | tf_op jit(solution)/shard_map/reduce_scatter | solution.py:286
  482.4 439.8 %reduce-scatter.22.cloned.1.call-start = ((), (), s32[]{:S(2)}) async-start(), calls=%async_computation.18 | async-start | bytes 8650752 | tf_op jit(solution)/shard_map/reduce_scatter | solution.py:280
  489.8 528.7 %reduce-scatter.26.cloned.1.call-start = ((), (), s32[]{:S(2)}) async-start(), calls=%async_computation.20 | async-start | bytes 8650752 | tf_op jit(solution)/shard_map/reduce_scatter | solution.py:292
  497.6 647.1 %all-reduce.14.cloned.1.call-start = ((), (), s32[]{:S(2)}) async-start(), calls=%async_computation.16 | async-start | bytes 2097152 | tf_op jit(solution)/shard_map/psum | solution.py:254
  497.6 57.0 %copy-start.25 = (f32[256,128]{1,0:T(8,128)S(1)}, f32[256,128]{1,0:T(8,128)}, u32[]{:S(2)}) copy-start(f32[256,128]{1,0:T(8,128)} %copy-done.24) | copy-start | bytes 393220
  497.6 57.0 %copy-start.30 = (f32[256,128]{1,0:T(8,128)S(1)}, f32[256,128]{1,0:T(8,128)}, u32[]{:S(2)}) copy-start(f32[256,128]{1,0:T(8,128)} %get-tuple-element.182) | copy-start | bytes 393220
  552.3 2.3 copy-start.15
  552.3 2.3 copy-start.22
  552.3 2.3 copy-start.23
  554.6 1.6 copy-start.9
  554.7 1.6 copy-start.37
  554.7 1.6 copy-start.39
  554.7 1.8 copy-start.11
  554.7 1.8 copy-start.35
  554.7 1.8 copy-start.41
  556.2 11.4 copy-start.45
  556.3 11.4 copy-start.43
  570.4 1.8 copy-start.20
  652.2 497.5 %reduce-scatter.30.cloned.1.call-start = ((), (), s32[]{:S(2)}) async-start(), calls=%async_computation.22 | async-start | bytes 2162688
  659.7 572.0 %reduce-scatter.28.cloned.1.call-start = ((), (), s32[]{:S(2)}) async-start(), calls=%async_computation.21 | async-start | bytes 2162688
  667.1 646.7 %reduce-scatter.32.cloned.1.call-start = ((), (), s32[]{:S(2)}) async-start(), calls=%async_computation.23 | async-start | bytes 2162688
  (6 other events, 5.1 us)
Sparse Core Ops, SparseCore 0:
  11.0 55.5 all-gather.4
  69.5 52.5 all-gather.2
  179.2 45.3 all-reduce.7
  242.6 46.6 all-reduce.9
  310.4 46.6 all-reduce.11
  458.7 93.5 reduce-scatter.15
  556.0 92.0 reduce-scatter.17
  652.0 78.2 reduce-scatter.19
  734.5 92.0 reduce-scatter.23
  830.1 92.0 reduce-scatter.21
  926.4 92.0 reduce-scatter.25
  1020.7 45.2 all-reduce.13
  1069.9 79.6 reduce-scatter.29
  1153.5 78.2 reduce-scatter.27
  1235.6 78.1 reduce-scatter.31
where the time goes:
time: 1330 us; the launch traced here: 1320 us
  waiting for transfers between devices  852 us (64%)
  matrix products  204 us (15%)
  blocking collectives  146 us (11%)
  other arithmetic  60.5 us (5%)
  local copies, waits for them, and re-layouts  42.2 us (3%)
  between operations  15 us (1%)
    unnamed x18, waiting for transfers between devices  162 us
    psum x1, blocking collectives, local(): lax.psum((local_q_gain, local_k_gain, local_attn_gain, local_mlp_gain), '...  124 us
    reduce_scatter x1, waiting for transfers between devices, local(): lax.psum_scatter(product_left(hidden_low, grad_up_proj).astype(jnp.bfloat...  94.7 us
    reduce_scatter x1, waiting for transfers between devices, local(): lax.psum_scatter(product_left(grad_down_proj, act_low).astype(jnp.bfloat1...  94.5 us
    reduce_scatter x1, waiting for transfers between devices, local(): lax.psum_scatter(product_left(hidden_low, grad_gate_proj).astype(jnp.bflo...  93.9 us
    reduce_scatter x1, waiting for transfers between devices, local(): lax.psum_scatter(value_total.astype(jnp.bfloat16), 'dp', scatter_dimensio...  73.8 us
    all_gather x1, waiting for transfers between devices, local(): key_piece = lax.all_gather(k_rot, 'dp', axis=0, tiled=True)  55.5 us
    reduce_scatter x1, waiting for transfers between devices, local(): lax.psum_scatter(product_left(grad_branch, mixed_low).astype(jnp.bfloat16...  55 us
  transfers between devices with their start and end apart: 15, of which 14 were waited for; matrix products, arithmetic and copies ran while one was open for 8% of the time, Pallas kernels for 0%

commit v1 on v0

v1 whole, which is shorter than its diff:
```python
import functools

import jax
import jax.numpy as jnp
from jax import lax
from jax.experimental import pallas as pl
from jax.experimental.pallas import tpu as pltpu
from jax.sharding import Mesh
from jax.sharding import PartitionSpec as P

HD = 128
HEADS = 4
TOK = 256
ROWS = 64
BLOCKS = 16
SEQ = 4096
WIDTH = 2048
epsilon = 1e-06
theta_base = 500000.0
weight_unit = 16.0
far_below = -1e30
score_scale = HD ** (-0.5)
LOG2E = 1.4426950408889634
F32 = jnp.float32
BF16 = jnp.bfloat16

FIRST = (1, 0, 3, 2)
SECOND = (3, 2, 1, 0)
VMEM_LIMIT = 48 * 1024 * 1024


def product(left, right):
    return jnp.dot(left, right, preferred_element_type=F32)


def product_right(left, right):
    return lax.dot_general(left, right, (((1,), (1,)), ((), ())), preferred_element_type=F32)


def product_left(left, right):
    return lax.dot_general(left, right, (((0,), (0,)), ((), ())), preferred_element_type=F32)


def swap(value, axis, pairing):
    return lax.ppermute(value, axis, [(i, pairing[i]) for i in range(4)])


def swap_core(value):
    return lax.ppermute(value, "c", [(0, 1), (1, 0)])


def swap_xz(value, x_pairing, z_pairing):
    pairs = [(i * 4 + j, x_pairing[i] * 4 + z_pairing[j]) for i in range(4) for j in range(4)]
    return lax.ppermute(value, ("x", "z"), pairs)


def shift_y(value, step):
    return lax.ppermute(value, "y", [(i, (i + step) % 4) for i in range(4)])


def scatter_y(partial):
    total = partial[:ROWS].astype(F32)
    for k in (1, 3, 2):
        total = total + shift_y(partial[k * ROWS : (k + 1) * ROWS], k).astype(F32)
    return total


def gather_y(own):
    received = {k: shift_y(own, -k) for k in (1, 3, 2)}
    return jnp.concatenate([own, received[1], received[2], received[3]], axis=0)


def sum_y(value):
    total = value
    for k in (1, 3, 2):
        total = total + jnp.roll(shift_y(value, k), -ROWS * k, axis=1)
    return total


def call(body, outs, operands, smem=1, scratch=(), cost=None):
    in_specs = [pl.BlockSpec(memory_space=pltpu.SMEM)] * smem
    in_specs += [pl.BlockSpec(memory_space=pltpu.VMEM)] * (len(operands) - smem)
    return pl.pallas_call(
        body,
        out_shape=[jax.ShapeDtypeStruct(s, d) for s, d in outs],
        in_specs=in_specs,
        out_specs=[pl.BlockSpec(memory_space=pltpu.VMEM)] * len(outs),
        scratch_shapes=list(scratch),
        compiler_params=pltpu.CompilerParams(vmem_limit_bytes=VMEM_LIMIT),
        cost_estimate=cost,
    )(*operands)


def attend_body(info, q_ref, kv0, kv1, kv2, kv3, qpos_ref, qstart_ref, o_ref, ot_ref, lse_ref, m_ref, l_ref, acc_ref):
    own_x = info[0]
    roll = info[1]
    kvs = (kv0, kv1, kv2, kv3)

    @pl.loop(0, 4)
    def _(a):
        block = info[2 + a]
        q = q_ref[a]
        qpos = qpos_ref[a]
        qstart = qstart_ref[a]
        m_ref[...] = jnp.full_like(m_ref, far_below)
        l_ref[...] = jnp.zeros_like(l_ref)
        acc_ref[...] = jnp.zeros_like(acc_ref)
        for xb in range(2):
            for group in range(4):
                at = 6 + (group * 2 + xb) * 2
                first, second = info[at], info[at + 1]

                @pl.when(jnp.minimum(first, second) <= block)
                def _(group=group, xb=xb, first=first, second=second):
                    start = (own_x ^ xb) * 2
                    k = kvs[group][0, pl.ds(start, 2)].reshape(2 * TOK, HD)
                    v = kvs[group][1, pl.ds(start, 2)].reshape(2 * TOK, HD)
                    s = product_right(k, q)
                    row = lax.broadcasted_iota(jnp.int32, (2 * TOK, TOK), 0)
                    place = ((row + roll) & (TOK - 1)) + jnp.where(row < TOK, first, second) * TOK
                    s = jnp.where((place <= qpos) & (place >= qstart), s, far_below)
                    m_old = m_ref[...]
                    m_new = jnp.maximum(m_old, jnp.max(s, axis=0, keepdims=True))
                    p = jnp.exp2((s - m_new) * (score_scale * LOG2E))
                    alpha = jnp.exp2((m_old - m_new) * (score_scale * LOG2E))
                    l_ref[...] = alpha * l_ref[...] + jnp.sum(p, axis=0, keepdims=True)
                    acc_ref[...] = alpha * acc_ref[...] + product_left(v, p.astype(BF16))
                    m_ref[...] = m_new

        out = acc_ref[...] / l_ref[...]
        ot_ref[a] = out
        o_ref[a] = out.T.astype(BF16)
        lse_ref[a] = m_ref[...] * (score_scale * LOG2E) + jnp.log2(l_ref[...])


def attend(info, q, kvs, qpos, qstart):
    return call(
        attend_body,
        [((4, TOK, HD), BF16), ((4, HD, TOK), F32), ((4, 1, TOK), F32)],
        [info, q, *kvs, qpos, qstart],
        scratch=[pltpu.VMEM((1, TOK), F32), pltpu.VMEM((1, TOK), F32), pltpu.VMEM((HD, TOK), F32)],
        cost=pl.CostEstimate(flops=36 * 4 * TOK * TOK * HD, bytes_accessed=4 << 20, transcendentals=36 * TOK * TOK),
    )


def attend_back_body(info, q_ref, kv0, kv1, kv2, kv3, qpos_ref, qstart_ref, do_ref, ot_ref, lse_ref, dq_ref, keep0_ref, keep2_ref, send_ref, acc_ref, dqt_ref):
    own_x = info[0]
    roll = info[1]
    kvs = (kv0, kv1, kv2, kv3)
    acc_ref[...] = jnp.zeros_like(acc_ref)

    @pl.loop(0, 4)
    def _(a):
        block = info[2 + a]
        q = q_ref[a]
        do = do_ref[a]
        delta = jnp.sum(do.astype(F32).T * ot_ref[a], axis=0, keepdims=True)
        lse = lse_ref[a]
        qpos = qpos_ref[a]
        qstart = qstart_ref[a]
        dqt_ref[...] = jnp.zeros_like(dqt_ref)
        for xb in range(2):
            for group in range(4):
                at = 6 + (group * 2 + xb) * 2
                first, second = info[at], info[at + 1]

                @pl.when(jnp.minimum(first, second) <= block)
                def _(group=group, xb=xb, first=first, second=second):
                    start = (own_x ^ xb) * 2
                    k = kvs[group][0, pl.ds(start, 2)].reshape(2 * TOK, HD)
                    v = kvs[group][1, pl.ds(start, 2)].reshape(2 * TOK, HD)
                    s = product_right(k, q)
                    dp = product_right(v, do)
                    row = lax.broadcasted_iota(jnp.int32, (2 * TOK, TOK), 0)
                    place = ((row + roll) & (TOK - 1)) + jnp.where(row < TOK, first, second) * TOK
                    keep = (place <= qpos) & (place >= qstart)
                    p = jnp.where(keep, jnp.exp2(s * (score_scale * LOG2E) - lse), 0.0)
                    ds = (p * (dp - delta)).astype(BF16)
                    dqt_ref[...] += product_left(k, ds)
                    acc_ref[group, 0, pl.ds(start, 2)] += product(ds, q).reshape(2, TOK, HD)
                    acc_ref[group, 1, pl.ds(start, 2)] += product(p.astype(BF16), do).reshape(2, TOK, HD)

        dq_ref[a] = (dqt_ref[...] * score_scale).T.astype(BF16)

    for group, out in ((0, keep0_ref), (2, keep2_ref), (1, send_ref.at[0]), (3, send_ref.at[1])):
        out[0] = (acc_ref[group, 0] * score_scale).astype(BF16)
        out[1] = acc_ref[group, 1].astype(BF16)


def attend_back(info, q, kvs, qpos, qstart, do, ot, lse):
    piece = (2, 4, TOK, HD)
    return call(
        attend_back_body,
        [((4, TOK, HD), BF16), (piece, BF16), (piece, BF16), ((2, *piece), BF16)],
        [info, q, *kvs, qpos, qstart, do, ot, lse],
        scratch=[pltpu.VMEM((4, *piece), F32), pltpu.VMEM((HD, TOK), F32)],
        cost=pl.CostEstimate(flops=36 * 10 * TOK * TOK * HD, bytes_accessed=8 << 20, transcendentals=36 * TOK * TOK),
    )


def enter_body(info, q_ref, k_ref, v_ref, rate_ref, gain_ref, cos_ref, sin_ref, *outs):
    head = info[0]
    cos, sin = cos_ref[...], sin_ref[...]
    for r in range(4):
        at = pl.ds(pl.multiple_of((head ^ r) * HD, HD), HD)
        for j, raw_ref in enumerate((q_ref, k_ref)):
            value = raw_ref[:, at] * rate_ref[j] * gain_ref[j, :, at]
            turned = pltpu.roll(value, HD // 2, 1)
            outs[r][j] = (value * cos + turned * sin).astype(BF16)
        outs[r][2] = v_ref[:, at]


def enter(info, q_raw, k_raw, v_low, rates, gains, cos, sin):
    return call(enter_body, [((3, TOK, HD), BF16)] * 4, [info, q_raw, k_raw, v_low, rates, gains, cos, sin])


def leave_body(info, q_ref, k_ref, rate_ref, gain_ref, cos_ref, sin_ref, *refs):
    head = info[0]
    dqs, dkvs = refs[:4], refs[4:8]
    q_scaled, k_scaled, v_low, gains_out, inner_out = refs[8:]
    cos, sin = cos_ref[...], sin_ref[...]
    inner = [jnp.zeros((TOK, 1), F32), jnp.zeros((TOK, 1), F32)]
    for r in range(4):
        at = pl.ds(pl.multiple_of((head ^ r) * HD, HD), HD)
        v_low[:, at] = dkvs[r][1]
        for j, (raw_ref, out) in enumerate(((q_ref, q_scaled), (k_ref, k_scaled))):
            grad = (dqs[r][...] if j == 0 else dkvs[r][0]).astype(F32)
            grad = grad * cos - pltpu.roll(grad, HD // 2, 1) * sin
            raw = raw_ref[:, at]
            gains_out[j, :, at] = jnp.sum(grad * raw * rate_ref[j], axis=0, keepdims=True)
            scaled = grad * gain_ref[j, :, at]
            out[:, at] = scaled
            inner[j] = inner[j] + jnp.sum(raw * scaled, axis=1, keepdims=True)
    for j in range(2):
        inner_out[j] = inner[j]


def leave(info, q_raw, k_raw, rates, gains, cos, sin, dqs, dkvs):
    outs = [((TOK, 512), F32), ((TOK, 512), F32), ((TOK, 512), BF16), ((2, 1, 512), F32), ((2, TOK, 1), F32)]
    return call(leave_body, outs, [info, q_raw, k_raw, rates, gains, cos, sin, *dqs, *dkvs])


def columns_body(info, x_ref, own_ref, other_ref):
    core = info[0]
    for k in range(BLOCKS):
        at = pl.ds(pl.multiple_of(info[1 + k] * 128, 128), 128)
        turned = x_ref[:, at].astype(F32).T
        low, high = turned[:ROWS], turned[ROWS:]
        own_ref[pl.ds(k * ROWS, ROWS)] = jnp.where(core == 0, low, high).astype(BF16)
        other_ref[pl.ds(k * ROWS, ROWS)] = jnp.where(core == 0, high, low).astype(BF16)


def columns(order, value):
    return call(columns_body, [((BLOCKS * ROWS, TOK), BF16)] * 2, [order, value])


def halves_body(bit, a0, a1, b0, b1, send_ref, keep_ref):
    rows = 256
    for i in range(BLOCKS * ROWS // rows):
        at = pl.ds(i * rows, rows)
        c = (product(a0[at], b0[...]) + product(a1[at], b1[...])).astype(BF16)
        for n in range(rows // ROWS):
            k = i * (rows // ROWS) + n
            upper = (k >> (3 - bit)) & 1
            low = k & ((1 << (3 - bit)) - 1)
            to = ((k >> (4 - bit)) << (3 - bit)) | low
            out = send_ref if upper else keep_ref
            out[pl.ds(to * ROWS, ROWS)] = c[n * ROWS : (n + 1) * ROWS]


def halves(bit, index, width, left, right):
    whole = pl.BlockSpec((BLOCKS * ROWS, TOK), lambda j: (0, 0))
    part = pl.BlockSpec((TOK, width), lambda j: (0, index))
    half = jax.ShapeDtypeStruct((BLOCKS * ROWS // 2, width), BF16)
    return pl.pallas_call(
        functools.partial(halves_body, bit),
        grid=(1,),
        out_shape=[half, half],
        in_specs=[whole, whole, part, part],
        out_specs=[pl.BlockSpec((BLOCKS * ROWS // 2, width), lambda j: (0, 0))] * 2,
        compiler_params=pltpu.CompilerParams(vmem_limit_bytes=VMEM_LIMIT),
        cost_estimate=pl.CostEstimate(flops=4 * BLOCKS * ROWS * TOK * width, bytes_accessed=BLOCKS * ROWS * width * 2, transcendentals=0),
    )(*left, *right)


STEPS = (("x", FIRST), ("x", SECOND), ("z", FIRST), ("z", SECOND))


def scatter_parts(pairs):
    bits = [[b for b in range(4) if b != p] for p in range(4)]
    sends = [s for s, _ in pairs]
    keeps = [k for _, k in pairs]
    for t in range(4):
        received = [swap(sends[p], *STEPS[(p + t) % 4]) for p in range(4)]
        if t == 3:
            return [(keeps[p].astype(F32) + received[p].astype(F32)) for p in range(4)]
        for p in range(4):
            bit = (p + t + 1) % 4
            at = bits[p].index(bit)
            bits[p].pop(at)
            width = keeps[p].shape[-1]
            shape = (1 << at, 2, (1 << (2 - t)) >> at, ROWS, width)
            kept, came = keeps[p].reshape(shape), received[p].reshape(shape)
            halves_now = [
                (kept[:, i].astype(F32) + came[:, i].astype(F32)).astype(BF16).reshape(-1, width) for i in (1, 0)
            ]
            sends[p], keeps[p] = halves_now


def plain_body(a0, a1, b0, b1, out):
    out[...] = (product(a0[...], b0[...]) + product(a1[...], b1[...])).astype(BF16)


def plain(left, right):
    columns_now = right[0].shape[1]
    width = min(512, columns_now)
    whole = pl.BlockSpec((BLOCKS * ROWS, TOK), lambda j: (0, 0))
    part = pl.BlockSpec((TOK, width), lambda j: (0, j))
    return pl.pallas_call(
        plain_body,
        grid=(columns_now // width,),
        out_shape=jax.ShapeDtypeStruct((BLOCKS * ROWS, columns_now), BF16),
        in_specs=[whole, whole, part, part],
        out_specs=pl.BlockSpec((BLOCKS * ROWS, width), lambda j: (0, j)),
        compiler_params=pltpu.CompilerParams(vmem_limit_bytes=VMEM_LIMIT),
        cost_estimate=pl.CostEstimate(flops=4 * BLOCKS * ROWS * TOK * columns_now, bytes_accessed=BLOCKS * ROWS * columns_now * 2, transcendentals=0),
    )(*left, *right)


def sum_all(value):
    for axis, pairing in STEPS:
        value = value + swap(value, axis, pairing)
    return value + swap_core(value)


def local(
    states,
    w_query,
    w_key,
    w_value,
    w_out,
    w_gate,
    w_up,
    w_down,
    q_gain,
    k_gain,
    attn_gain,
    mlp_gain,
    cotangent,
    segments,
    sources,
    group_weights,
):
    x, z, c, y = (lax.axis_index(n) for n in ("x", "z", "c", "y"))
    own_x = x & 1
    z_low, z_high = (z ^ (z >> 1)) & 1, z >> 1
    head = own_x * 2 + z_high
    roll = y * ROWS
    head_info = head.reshape(1)

    def rolled(value):
        return lax.dynamic_slice_in_dim(jnp.concatenate([value, value], axis=0), roll, TOK, 0)

    def own_rows(value):
        return lax.dynamic_slice_in_dim(value, roll, ROWS, 0)

    here = (jnp.arange(TOK, dtype=jnp.int32) + roll) & (TOK - 1)
    own_block = own_x * 8 + z * 2 + c

    def z_of(high, low):
        return high * 2 + (low ^ high)

    q_blocks = jnp.stack([(own_x ^ (a >> 1)) * 8 + z_of(z_high ^ (a & 1), z_low) * 2 + c for a in range(4)])
    tiles = []
    for group in range(4):
        for xb in range(2):
            for a in range(2):
                tiles.append(xb * 8 + z_of(z_high ^ a, z_low ^ (group >> 1)) * 2 + (c ^ (group & 1)))
    info = jnp.stack([own_x, roll, *q_blocks, *tiles]).astype(jnp.int32)
    q_pos = q_blocks[:, None] * TOK + here[None]
    seq_segments = lax.dynamic_slice_in_dim(segments, (x >> 1) * SEQ, SEQ)
    q_segments = seq_segments[q_pos.reshape(-1)]
    q_start = jnp.sum((seq_segments[None, :] < q_segments[:, None]).astype(jnp.int32), axis=1)
    q_start = q_start.reshape(4, 1, TOK)
    q_pos = q_pos.reshape(4, 1, TOK)

    inverse = 1.0 / theta_base ** (jnp.arange(0, HD, 2, dtype=F32) / HD)
    angles = (own_block * TOK + here).astype(F32)[:, None] * inverse[None, :]
    cosine, sine = jnp.cos(angles), jnp.sin(angles)
    cos_table = jnp.concatenate([cosine, cosine], axis=-1)
    sin_table = jnp.concatenate([-sine, sine], axis=-1)
    gains = jnp.stack([q_gain, k_gain]).reshape(2, 1, 512)

    states_here = rolled(states)
    query_raw = product(states_here, w_query)
    key_raw = product(states_here, w_key)
    value_low = product(states_here, w_value).astype(BF16)
    squares = jnp.stack([jnp.sum(query_raw * query_raw, axis=1), jnp.sum(key_raw * key_raw, axis=1)])
    squares = sum_y(squares)
    rates = lax.rsqrt(squares / WIDTH + epsilon)
    rates_column = rates.reshape(2, TOK, 1)
    mine, to_z, to_x, to_xz = enter(head_info, query_raw, key_raw, value_low, rates_column, gains, cos_table, sin_table)

    def exchange(to_z, to_x, to_xz):
        return swap(to_z, "z", SECOND), swap(to_x, "x", FIRST), swap_xz(to_xz, FIRST, SECOND)

    pieces = jnp.stack([mine, *exchange(to_z, to_x, to_xz)], axis=1)
    q_here, kv_own = pieces[0], pieces[1:]
    kv_z = swap(kv_own, "z", FIRST)
    kv_c = swap_core(kv_own)
    kv_zc = swap_core(kv_z)
    kvs = (kv_own, kv_c, kv_z, kv_zc)
    mixed, mixed_turned, log_total = attend(info, q_here, kvs, q_pos, q_start)
    back = jnp.stack([mixed[0], *exchange(mixed[1], mixed[2], mixed[3])])
    mixed_low = jnp.concatenate([lax.dynamic_index_in_dim(back, head ^ k, 0, False) for k in range(4)], axis=1)

    branch = scatter_y(product(mixed_low, w_out).astype(BF16))
    b_rate = lax.rsqrt(jnp.mean(branch * branch, axis=1, keepdims=True) + epsilon)
    b_norm = branch * b_rate
    hidden = own_rows(states).astype(F32) + attn_gain * b_norm
    hidden_low = gather_y(hidden.astype(BF16))
    gate_proj = product(hidden_low, w_gate)
    up_proj = product(hidden_low, w_up)
    sigmoid_gate = jax.nn.sigmoid(gate_proj)
    silu_gate = gate_proj * sigmoid_gate
    act_low = (silu_gate * up_proj).astype(BF16)
    down_proj = scatter_y(product(act_low, w_down).astype(BF16))
    d_rate = lax.rsqrt(jnp.mean(down_proj * down_proj, axis=1, keepdims=True) + epsilon)
    d_norm = down_proj * d_rate
    output_own = (hidden + mlp_gain * d_norm).astype(BF16)

    chosen = own_rows(sources)[:, None] == jnp.arange(group_weights.shape[0], dtype=jnp.int32)[None, :]
    token_share = jnp.sum(jnp.where(chosen, group_weights[None, :], 0), axis=1).astype(F32) / weight_unit
    grad_top = own_rows(cotangent).astype(F32) * token_share[:, None]
    local_mlp_gain = jnp.sum(grad_top * d_norm, axis=0)
    scaled_top = mlp_gain * grad_top
    grad_down_own = (
        d_rate * (scaled_top - d_norm * jnp.mean(scaled_top * d_norm, axis=1, keepdims=True))
    ).astype(BF16)
    grad_down_proj = gather_y(grad_down_own)

    x_order = [x, jnp.bitwise_xor(x, 1), 3 - x, 3 - jnp.bitwise_xor(x, 1)]
    z_order = [z, jnp.bitwise_xor(z, 1), 3 - z, 3 - jnp.bitwise_xor(z, 1)]
    by_bits = (0, 2, 1, 3)
    order = jnp.stack([c] + [x_order[by_bits[i]] * 4 + z_order[by_bits[j]] for i in range(4) for j in range(4)])
    plain_order = jnp.concatenate([c.reshape(1), jnp.arange(BLOCKS, dtype=jnp.int32)])

    def shared(order_now, left, rights):
        own, other = columns(order_now, left)
        return (own, swap_core(other)), [(r, swap_core(r)) for r in rights]

    down_left, (down_right,) = shared(plain_order, grad_down_proj, [act_low])
    grad_down = lax.psum_scatter(plain(down_left, down_right), ("x", "z"), scatter_dimension=0, tiled=True)

    grad_act = product_right(grad_down_proj, w_down)
    grad_gate_proj = (grad_act * up_proj * sigmoid_gate * (1.0 + gate_proj * (1.0 - sigmoid_gate))).astype(BF16)
    grad_up_proj = (grad_act * silu_gate).astype(BF16)
    hidden_part = product_right(grad_gate_proj, w_gate) + product_right(grad_up_proj, w_up)
    hidden_sum = scatter_y(hidden_part.astype(BF16))

    gate_left, (gate_right, up_right) = shared(order, hidden_low, [grad_gate_proj, grad_up_proj])
    gate_up = scatter_parts(
        [
            halves(0, 0, 1024, gate_left, gate_right),
            halves(1, 1, 1024, gate_left, gate_right),
            halves(2, 0, 1024, gate_left, up_right),
            halves(3, 1, 1024, gate_left, up_right),
        ]
    )
    output = gather_y(output_own)

    grad_hidden = grad_top + hidden_sum
    local_attn_gain = jnp.sum(grad_hidden * b_norm, axis=0)
    scaled_hidden = attn_gain * grad_hidden
    grad_branch = gather_y(
        (b_rate * (scaled_hidden - b_norm * jnp.mean(scaled_hidden * b_norm, axis=1, keepdims=True))).astype(BF16)
    )
    grad_mixed = product_right(grad_branch, w_out).astype(BF16)
    to = [lax.dynamic_slice_in_dim(grad_mixed, (head ^ r) * HD, HD, 1) for r in range(4)]
    grad_mixed_here = jnp.stack([to[0], *exchange(to[1], to[2], to[3])])

    out_left, (out_right,) = shared(plain_order, grad_branch, [mixed_low])
    grad_out = lax.psum_scatter(plain(out_left, out_right), ("x", "z"), scatter_dimension=0, tiled=True)

    dq, keep_own, keep_z, send_c = attend_back(
        info, q_here, kvs, q_pos, q_start, grad_mixed_here, mixed_turned, log_total
    )
    dqs = [dq[0], *exchange(dq[1], dq[2], dq[3])]
    came = swap_core(send_c)
    keep_z = (keep_z.astype(F32) + came[1].astype(F32)).astype(BF16)
    keep_own = keep_own.astype(F32) + came[0].astype(F32)
    keep_own = (keep_own + swap(keep_z, "z", FIRST).astype(F32)).astype(BF16)
    dkvs = [keep_own[:, 0], *exchange(keep_own[:, 1], keep_own[:, 2], keep_own[:, 3])]
    q_scaled, k_scaled, grad_value_low, local_qk_gain, inner = leave(
        head_info, query_raw, key_raw, rates_column, gains, cos_table, sin_table, dqs, dkvs
    )
    inner = inner.reshape(2, TOK)
    inner = sum_y(inner)
    factor = rates * rates * rates * inner / WIDTH
    grad_query_raw = (rates[0][:, None] * q_scaled - query_raw * factor[0][:, None]).astype(BF16)
    grad_key_raw = (rates[1][:, None] * k_scaled - key_raw * factor[1][:, None]).astype(BF16)
    input_part = (
        product_right(grad_query_raw, w_query)
        + product_right(grad_key_raw, w_key)
        + product_right(grad_value_low, w_value)
    )
    grad_states_own = grad_hidden + scatter_y(input_part.astype(BF16))
    grad_states = gather_y(grad_states_own.astype(BF16))

    together = jnp.concatenate([grad_query_raw, grad_key_raw, grad_value_low], axis=1)
    qkv_left, (qkv_right,) = shared(order, states_here, [together])
    qkv = jnp.concatenate(scatter_parts([halves(p, p, 384, qkv_left, qkv_right) for p in range(4)]), axis=1)

    wide_gains = sum_all(jnp.stack([local_attn_gain, local_mlp_gain]))
    wide_gains = wide_gains + swap(wide_gains, "y", FIRST)
    wide_gains = wide_gains + swap(wide_gains, "y", SECOND)
    qk_gains = sum_all(local_qk_gain.reshape(2, 512))

    def unrolled(value):
        return lax.dynamic_slice_in_dim(jnp.concatenate([value, value], axis=0), (TOK - roll) & (TOK - 1), TOK, 0)

    return (
        unrolled(output),
        unrolled(grad_states).astype(F32),
        qkv[:, :512],
        qkv[:, 512:1024],
        qkv[:, 1024:],
        jnp.transpose(grad_out.astype(F32)),
        jnp.concatenate(gate_up[:2], axis=1),
        jnp.concatenate(gate_up[2:], axis=1),
        jnp.transpose(grad_down.astype(F32)),
        qk_gains[0],
        qk_gains[1],
        wide_gains[0],
        wide_gains[1],
    )


def solution(mesh):
    split = Mesh(mesh.devices.reshape(4, 4, 2, 4), ("x", "z", "c", "y"))
    dp, mp = ("x", "z", "c"), "y"
    placed = (
        P(dp, None),
        P(None, mp),
        P(None, mp),
        P(None, mp),
        P(mp, None),
        P(None, mp),
        P(None, mp),
        P(mp, None),
        P(mp),
        P(mp),
        P(),
        P(),
        P(dp, None),
        P(),
        P(dp),
        P(),
    )
    return jax.shard_map(
        local,
        mesh=split,
        in_specs=placed,
        out_specs=(
            P(dp, None),
            P(dp, None),
            P(dp, mp),
            P(dp, mp),
            P(dp, mp),
            P(mp, dp),
            P(dp, mp),
            P(dp, mp),
            P(mp, dp),
            P(mp),
            P(mp),
            P(),
            P(),
        ),
        check_vma=False,
    )
```

time: 1330 us -> 497 us (0.37)
  waiting for transfers between devices: 852 us -> 165 us
  matrix products: 204 us -> 45.8 us
  blocking collectives: 146 us -> 0 us
  starting transfers between devices: 1.38 us -> 123 us
  Pallas kernels: 0 us -> 57.9 us
  other arithmetic: 60.5 us -> 44.5 us
    reduce_scatter x6 -> x2, waiting for transfers between devices: 464 us -> 0.01 us  [the longest x1 0.01 us: local(): lax.psum_scatter(plain(out_left, out_right), ('x', 'z'), scatter_dimensio...]
    ppermute x0 -> x106, waiting for transfers between devices: none -> 165 us  [the longest x54 80.1 us: swap(): return lax.ppermute(value, axis, [(i, pairing[i]) for i in range(4)])]
    unnamed x18 -> x2, waiting for transfers between devices: 162 us -> 0.03 us
    psum x3 -> x0, blocking collectives: 146 us -> none  [the longest x1 124 us: local(): lax.psum((local_q_gain, local_k_gain, local_attn_gain, local_mlp_gain), '...]
    dot_general x20 -> x7, matrix products: 161 us -> 21.7 us  [product(): return jnp.dot(left, right, preferred_element_type=F32)]
    psum x4 -> x0, waiting for transfers between devices: 138 us -> none  [the longest x1 46.7 us: local(): lax.psum(hidden_part.astype(jnp.bfloat16), 'mp').astype(jnp.float32)]
    ppermute x0 -> x106, starting transfers between devices: none -> 122 us  [the longest x54 64.7 us: swap(): return lax.ppermute(value, axis, [(i, pairing[i]) for i in range(4)])]
    all_gather x2 -> x0, waiting for transfers between devices: 87.6 us -> none  [the longest x1 55.5 us: local(): key_piece = lax.all_gather(k_rot, 'dp', axis=0, tiled=True)]
  transfers between devices with their start and end apart: 15 -> 108, of which waited for: 14 -> 51; matrix products, arithmetic and copies ran while one was open for 8% -> 17% of each run, Pallas kernels for 0% -> 9%
where the time goes in v1:
time: 497 us; the launch traced here: 488 us
  waiting for transfers between devices  165 us (33%)
  starting transfers between devices  123 us (25%)
  Pallas kernels  57.9 us (12%)
  matrix products  45.8 us (9%)
  other arithmetic  44.5 us (9%)
  local copies, waits for them, and re-layouts  36.7 us (7%)
  between operations  16.3 us (3%)
    ppermute x54, waiting for transfers between devices, swap(): return lax.ppermute(value, axis, [(i, pairing[i]) for i in range(4)])  80.1 us
    ppermute x33, waiting for transfers between devices, shift_y(): return lax.ppermute(value, 'y', [(i, (i + step) % 4) for i in range(4)])  69 us
    ppermute x54, starting transfers between devices, swap(): return lax.ppermute(value, axis, [(i, pairing[i]) for i in range(4)])  64.7 us
    ppermute x33, starting transfers between devices, shift_y(): return lax.ppermute(value, 'y', [(i, (i + step) % 4) for i in range(4)])  47.5 us
    pallas_call x8, Pallas kernels, call(): pl.pallas_call(body, out_shape=[jax.ShapeDtypeStruct(s, d) for s, d in ou...  34.4 us
    dot_general x7, matrix products, product_right(): lax.dot_general(left, right, (((1,), (1,)), ((), ())), preferred_element_...  24.1 us
    dot_general x7, matrix products, product(): return jnp.dot(left, right, preferred_element_type=F32)  21.7 us
    pallas_call x8, Pallas kernels, halves(): pl.pallas_call(functools.partial(halves_body, bit), grid=(1,), out_shape=...  18.4 us
  transfers between devices with their start and end apart: 108, of which 51 were waited for; matrix products, arithmetic and copies ran while one was open for 17% of the time, Pallas kernels for 9%

profile of v1, /device:TPU:0, one launch (start us, length us, event | category | flops | bytes accessed | tf_op | source)
XLA Modules:
  0.0 488.3 jit_solution(15594634268203255092)
XLA Ops:
  7.2 2.2 fusion.3.x_ref
  12.9 3.3 collective-permute-start.2
  16.8 2.6 collective-permute-start.1
  19.4 3.3 convolution_convert_fusion.3.v_ref
  33.9 4.1 collective-permute-start.3
  39.7 2.7 collective-permute-done.3
  42.4 3.3 collective-permute-done.4
  48.0 11.9 %collective-permute-done.7.kv2 = bf16[2,4,256,128]{3,2,1,0:T(8,128)(2,1)} collective-permute-done((bf16[2,4,256,128]{3,2,1,0:T(8,128)(2,1)S(1)}, bf16[2,4,256,128]{3,2,1,0:T(8,128)(2,1)}, u32[]{:S(2)}, u32[]{:S(2)}) %collective-permute-start.7) | collective-permute-done | bytes 524320 | tf_op jit(solution)/shard_map/ppermute | solution.py:45
  60.9 6.1 %gather_fusion = s32[1024]{0:T(1024)S(1)} fusion(s32[4096]{0:T(1024)S(1)} %dynamic_slice.48, s32[1024]{0:T(1024)S(1)} %broadcast_clamp_fusion), kind=kCustom, calls=%fused_computation | custom fusion | bytes 12288 | tf_op jit(solution)/shard_map/gather | solution.py:382
  69.9 11.9 %shard_map.256 = (bf16[4,256,128]{2,1,0:T(8,128)(2,1)S(1)}, f32[4,128,256]{2,1,0:T(8,128)S(1)}, f32[4,1,256]{2,1,0:T(1,128)S(1)}) custom-call(s32[22]{0:T(128)S(1)} %stack.223.info, bf16[4,256,128]{2,1,0:T(8,128)(2,1)S(1)} %maximum_bitcast_fusion.q_ref, bf16[2,4,256,128]{3,2,1,0:T(8,128)(2,1)S(1)} %pad_maximum_fusion.4.kv0, ...), custom_call_target="tpu_custom_call" | custom-call | flops 1207959552 | bytes 4194304 | tf_op jit(solution)/shard_map/pallas_call | solution.py:83
  89.4 3.9 collective-permute-done.11
  93.4 2.4 convolution_convert_fusion
  97.0 3.2 collective-permute-start.13
  100.4 12.0 %collective-permute-done.12 = bf16[64,2048]{1,0:T(8,128)(2,1)S(1)} collective-permute-done((bf16[64,2048]{1,0:T(8,128)(2,1)}, bf16[64,2048]{1,0:T(8,128)(2,1)S(1)}, u32[]{:S(2)}, u32[]{:S(2)}) %collective-permute-start.12) | collective-permute-done | bytes 262176 | tf_op jit(solution)/shard_map/ppermute | solution.py:58
  115.0 3.0 collective-permute-start.15
  122.5 5.8 %collective-permute-done.15 = bf16[64,2048]{1,0:T(8,128)(2,1)} collective-permute-done((bf16[64,2048]{1,0:T(8,128)(2,1)S(1)}, bf16[64,2048]{1,0:T(8,128)(2,1)}, u32[]{:S(2)}, u32[]{:S(2)}) %collective-permute-start.15) | collective-permute-done | bytes 262176 | tf_op jit(solution)/shard_map/ppermute | solution.py:58
  128.8 3.3 collective-permute-done.17
  132.1 6.1 %fusion.55 = f32[256,2048]{1,0:T(8,128)S(1)} fusion(bf16[2048,2048]{1,0:T(8,128)(2,1)} %param.21, bf16[64,2048]{1,0:T(8,128)(2,1)} %collective-permute-done.17, bf16[64,2048]{1,0:T(8,128)(2,1)} %collective-permute-done.16, bf16[64,2048]{1,0:T(8,128)(2,1)} %collective-permute-done.15, bf16[64,2048]{1,0:T(8,128)(2,1)S(1)} %fusion.9), kind=kOutput, calls=%fused_computation.245 | convolution fusion | flops 2151677952 | bytes 11534336 | tf_op jit(solution)/shard_map/dot_general | solution.py:33
  138.3 5.9 %multiply_convert_fusion.2 = (bf16[256,2048]{1,0:T(8,128)(2,1)S(1)}, f32[256,2048]{1,0:T(8,128)}) fusion(f32[256,2048]{1,0:T(8,128)S(1)} %fusion.55, bf16[2048,2048]{1,0:T(8,128)(2,1)S(1)} %bitcast.432, bf16[64,2048]{1,0:T(8,128)(2,1)} %collective-permute-done.17, bf16[64,2048]{1,0:T(8,128)(2,1)} %collective-permute-done.16, ...), kind=kOutput, calls=%fused_computation.13 | convolution fusion | flops 2154823680 | bytes 14680064 | tf_op jit(solution)/shard_map/dot_general | solution.py:33
  144.3 2.4 convolution_convert_fusion.1
  146.8 3.2 collective-permute-start.19
  153.8 8.1 %collective-permute-done.18 = bf16[64,2048]{1,0:T(8,128)(2,1)S(1)} collective-permute-done((bf16[64,2048]{1,0:T(8,128)(2,1)S(1)}, bf16[64,2048]{1,0:T(8,128)(2,1)S(1)}, u32[]{:S(2)}, u32[]{:S(2)}) %collective-permute-start.18) | collective-permute-done | bytes 262176 | tf_op jit(solution)/shard_map/ppermute | solution.py:58
  162.7 3.0 collective-permute-start.24
  167.8 8.8 %collective-permute-done.24 = bf16[64,2048]{1,0:T(8,128)(2,1)S(1)} collective-permute-done((bf16[64,2048]{1,0:T(8,128)(2,1)S(1)}, bf16[64,2048]{1,0:T(8,128)(2,1)S(1)}, u32[]{:S(2)}, u32[]{:S(2)}) %collective-permute-start.24) | collective-permute-done | bytes 262176 | tf_op jit(solution)/shard_map/ppermute | solution.py:58
  176.7 3.9 collective-permute-start.21
  181.7 7.7 %multiply_convert_fusion = (bf16[256,2048]{1,0:T(8,128)(2,1)}, bf16[256,2048]{1,0:T(8,128)(2,1)}) fusion(f32[256,2048]{1,0:T(8,128)S(1)} %copy-done.103, f32[256,2048]{1,0:T(8,128)S(1)} %copy-done.104, bf16[2048,2048]{1,0:T(8,128)(2,1)} %param.23, bf16[64,2048]{1,0:T(8,128)(2,1)S(1)} %collective-permute-done.26, ...), kind=kOutput, calls=%fused_computation.11 | convolution fusion | flops 2158493696 | bytes 15728640 | tf_op jit(solution)/shard_map/dot_general | solution.py:37
  189.4 6.1 %fusion.71 = f32[256,2048]{1,0:T(8,128)S(1)} fusion(bf16[256,2048]{1,0:T(8,128)(2,1)} %get-tuple-element.109.b0, bf16[2048,2048]{1,0:T(8,128)(2,1)} %param.21), kind=kOutput, calls=%fused_computation.261 | convolution fusion | flops 2147483648 | bytes 11534336 | tf_op jit(solution)/shard_map/dot_general | solution.py:37
  195.5 6.1 %fusion = bf16[256,2048]{1,0:T(8,128)(2,1)S(1)} fusion(f32[256,2048]{1,0:T(8,128)S(1)} %fusion.71, bf16[256,2048]{1,0:T(8,128)(2,1)} %get-tuple-element.108.b0, bf16[2048,2048]{1,0:T(8,128)(2,1)} %param.22), kind=kOutput, calls=%fused_computation.5 | convolution fusion | flops 2148532224 | bytes 12582912 | tf_op jit(solution)/shard_map/dot_general | solution.py:37
  201.7 2.6 collective-permute-start.27
  206.6 4.6 collective-permute-done.27
  211.2 4.1 collective-permute-done.28
  218.1 3.2 collective-permute-done.99
  221.3 2.2 collective-permute-start.100
  227.7 4.2 collective-permute-done.30
  232.0 2.3 collective-permute-done.31
  239.9 3.5 collective-permute-done.102
  248.0 2.5 constant_dynamic-slice_fusion.3
  257.1 2.5 collective-permute-start.35
  261.3 2.3 collective-permute-done.35
  263.7 14.8 %shard_map.257 = (bf16[4,256,128]{2,1,0:T(8,128)(2,1)S(1)}, bf16[2,4,256,128]{3,2,1,0:T(8,128)(2,1)S(1)}, bf16[2,4,256,128]{3,2,1,0:T(8,128)(2,1)S(1)}, bf16[2,2,4,256,128]{4,3,2,1,0:T(8,128)(2,1)S(1)}) custom-call(s32[22]{0:T(128)S(1)} %stack.223.info, bf16[4,256,128]{2,1,0:T(8,128)(2,1)S(1)} %copy-done.38, bf16[2,4,256,128]{3,2,1,0:T(8,128)(2,1)S(1)} %copy-done.24, ...), custom_call_target="tpu_custom_call" | custom-call | flops 3019898880 | bytes 8388608 | tf_op jit(solution)/shard_map/pallas_call | solution.py:83
  281.4 3.6 shard_map.269
  287.5 3.7 shard_map.270
  293.8 4.4 shard_map.272
  299.3 2.7 shard_map.267
  304.7 2.6 shard_map.268
  309.9 3.3 collective-permute-done.84
  313.9 2.6 add_convert_fusion.3
  316.5 4.3 collective-permute-done.88
  321.1 2.7 add_convert_fusion.1
  323.8 4.9 %collective-permute-done.75 = bf16[512,1024]{1,0:T(8,128)(2,1)S(1)} collective-permute-done((bf16[512,1024]{1,0:T(8,128)(2,1)S(1)}, bf16[512,1024]{1,0:T(8,128)(2,1)S(1)}, u32[]{:S(2)}, u32[]{:S(2)}) %collective-permute-start.75) | collective-permute-done | bytes 1048608 | tf_op jit(solution)/shard_map/ppermute | solution.py:45
  337.8 4.2 collective-permute-done.79
  344.2 5.1 %collective-permute-done.43.refs_7_ = bf16[2,256,128]{2,1,0:T(8,128)(2,1)S(1)} collective-permute-done((bf16[2,256,128]{2,1,0:T(8,128)(2,1)S(1)}, bf16[2,256,128]{2,1,0:T(8,128)(2,1)S(1)}, u32[]{:S(2)}, u32[]{:S(2)}) %collective-permute-start.43) | collective-permute-done | bytes 131104 | tf_op jit(solution)/shard_map/ppermute | solution.py:54
  358.6 2.8 collective-permute-start.45
  367.9 3.8 collective-permute-done.95
  372.5 2.8 collective-permute-done.96
  388.6 14.0 %collective-permute-done.85 = bf16[256,1024]{1,0:T(8,128)(2,1)S(1)} collective-permute-done((bf16[256,1024]{1,0:T(8,128)(2,1)S(1)}, bf16[256,1024]{1,0:T(8,128)(2,1)S(1)}, u32[]{:S(2)}, u32[]{:S(2)}) %collective-permute-start.85) | collective-permute-done | bytes 524320 | tf_op jit(solution)/shard_map/ppermute | solution.py:45
  405.0 2.2 collective-permute-start.51
  407.7 5.6 %collective-permute-done.50 = bf16[64,2048]{1,0:T(8,128)(2,1)S(1)} collective-permute-done((bf16[64,2048]{1,0:T(8,128)(2,1)S(1)}, bf16[64,2048]{1,0:T(8,128)(2,1)S(1)}, u32[]{:S(2)}, u32[]{:S(2)}) %collective-permute-start.50) | collective-permute-done | bytes 262176 | tf_op jit(solution)/shard_map/ppermute | solution.py:58
  415.8 2.8 collective-permute-start.90
  423.4 2.8 collective-permute-start.87
  428.2 2.6 collective-permute-done.81
  432.9 4.1 collective-permute-done.78
  443.7 2.5 collective-permute-start.59
  468.5 2.4 collective-permute-start.69
  (554 shorter events, 184.8 us)
Async XLA Ops:
  7.2 444.7 %reduce-scatter.3.cloned.1.call-start = ((), (), s32[]{:S(2)}) async-start(), calls=%async_computation.2 | async-start | bytes 1114112 | tf_op jit(solution)/shard_map/reduce_scatter | solution.py:483
  12.9 15.1 %collective-permute-start.2 = (f32[2,256]{1,0:T(2,128)}, f32[2,256]{1,0:T(2,128)}, u32[]{:S(2)}, u32[]{:S(2)}) collective-permute-start(f32[2,256]{1,0:T(2,128)} %pad_maximum_fusion.19), channel_id=1, source_target_pairs={{0,2},{1,3},{2,0},{3,1},{4,6},{5,7},{6,4},{7,5},{8,10},{9,11},{10,... | collective-permute-start | bytes 6152 | tf_op jit(solution)/shard_map/ppermute | solution.py:58
  16.8 9.9 %collective-permute-start.1 = (f32[2,256]{1,0:T(2,128)}, f32[2,256]{1,0:T(2,128)S(1)}, u32[]{:S(2)}, u32[]{:S(2)}) collective-permute-start(f32[2,256]{1,0:T(2,128)} %pad_maximum_fusion.19), channel_id=1, source_target_pairs={{0,3},{1,0},{2,1},{3,2},{4,7},{5,4},{6,5},{7,6},{8,11},{9,8},{10,9... | collective-permute-start | bytes 6152 | tf_op jit(solution)/shard_map/ppermute | solution.py:58
  33.9 8.4 %collective-permute-start.3 = (bf16[3,256,128]{2,1,0:T(8,128)(2,1)S(1)}, bf16[3,256,128]{2,1,0:T(8,128)(2,1)S(1)}, u32[]{:S(2)}, u32[]{:S(2)}) collective-permute-start(bf16[3,256,128]{2,1,0:T(8,128)(2,1)S(1)} %get-tuple-element.54), channel_id=1, source_target_pairs={{0,24},{8,16},{16,8},{24,0},{1,25},{9,17},{17,9},{25,1},{2,26},{10... | collective-permute-start | bytes 589832 | tf_op jit(solution)/shard_map/ppermute | solution.py:45
  47.7 12.2 %collective-permute-start.7 = (bf16[2,4,256,128]{3,2,1,0:T(8,128)(2,1)S(1)}, bf16[2,4,256,128]{3,2,1,0:T(8,128)(2,1)}, u32[]{:S(2)}, u32[]{:S(2)}) collective-permute-start(bf16[2,4,256,128]{3,2,1,0:T(8,128)(2,1)S(1)} %pad_maximum_fusion.4.kv0), channel_id=1, source_target_pairs={{0,8},{8,0},{16,24},{24,16},{1,9},{9,1},{17,25},{25,17},{2,10},{10... | collective-permute-start | bytes 1572872 | tf_op jit(solution)/shard_map/ppermute | solution.py:45
  47.9 22.0 %collective-permute-start.6 = (bf16[2,4,256,128]{3,2,1,0:T(8,128)(2,1)S(1)}, bf16[2,4,256,128]{3,2,1,0:T(8,128)(2,1)}, u32[]{:S(2)}, u32[]{:S(2)}) collective-permute-start(bf16[2,4,256,128]{3,2,1,0:T(8,128)(2,1)S(1)} %pad_maximum_fusion.4.kv0), channel_id=1, source_target_pairs={{0,4},{4,0},{1,5},{5,1},{2,6},{6,2},{3,7},{7,3},{8,12},{12,8},{9,1... | collective-permute-start | bytes 1572872 | tf_op jit(solution)/shard_map/ppermute | solution.py:49
  59.9 10.0 %collective-permute-start.8 = (bf16[2,4,256,128]{3,2,1,0:T(8,128)(2,1)}, bf16[2,4,256,128]{3,2,1,0:T(8,128)(2,1)}, u32[]{:S(2)}, u32[]{:S(2)}) collective-permute-start(bf16[2,4,256,128]{3,2,1,0:T(8,128)(2,1)} %collective-permute-done.7.kv2), channel_id=1, source_target_pairs={{0,4},{4,0},{1,5},{5,1},{2,6},{6,2},{3,7},{7,3},{8,12},{12,8},{9,1... | collective-permute-start | bytes 1572872 | tf_op jit(solution)/shard_map/ppermute | solution.py:49
  97.0 15.4 %collective-permute-start.12 = (bf16[64,2048]{1,0:T(8,128)(2,1)}, bf16[64,2048]{1,0:T(8,128)(2,1)S(1)}, u32[]{:S(2)}, u32[]{:S(2)}) collective-permute-start(bf16[64,2048]{1,0:T(8,128)(2,1)} %get-tuple-element.134), channel_id=1, source_target_pairs={{0,1},{1,2},{2,3},{3,0},{4,5},{5,6},{6,7},{7,4},{8,9},{9,10},{10,1... | collective-permute-start | bytes 786440 | tf_op jit(solution)/shard_map/ppermute | solution.py:58
  97.0 15.4 %collective-permute-start.13 = (bf16[64,2048]{1,0:T(8,128)(2,1)}, bf16[64,2048]{1,0:T(8,128)(2,1)S(1)}, u32[]{:S(2)}, u32[]{:S(2)}) collective-permute-start(bf16[64,2048]{1,0:T(8,128)(2,1)} %get-tuple-element.136), channel_id=1, source_target_pairs={{0,3},{1,0},{2,1},{3,2},{4,7},{5,4},{6,5},{7,6},{8,11},{9,8},{10,9... | collective-permute-start | bytes 786440 | tf_op jit(solution)/shard_map/ppermute | solution.py:58
  100.2 12.1 %collective-permute-start.14 = (bf16[64,2048]{1,0:T(8,128)(2,1)S(1)}, bf16[64,2048]{1,0:T(8,128)(2,1)}, u32[]{:S(2)}, u32[]{:S(2)}) collective-permute-start(bf16[64,2048]{1,0:T(8,128)(2,1)S(1)} %get-tuple-element.135), channel_id=1, source_target_pairs={{0,2},{1,3},{2,0},{3,1},{4,6},{5,7},{6,4},{7,5},{8,10},{9,11},{10,... | collective-permute-start | bytes 786440 | tf_op jit(solution)/shard_map/ppermute | solution.py:58
  115.0 13.3 %collective-permute-start.15 = (bf16[64,2048]{1,0:T(8,128)(2,1)S(1)}, bf16[64,2048]{1,0:T(8,128)(2,1)}, u32[]{:S(2)}, u32[]{:S(2)}) collective-permute-start(bf16[64,2048]{1,0:T(8,128)(2,1)S(1)} %fusion.9), channel_id=1, source_target_pairs={{0,3},{1,0},{2,1},{3,2},{4,7},{5,4},{6,5},{7,6},{8,11},{9,8},{10,9... | collective-permute-start | bytes 786440 | tf_op jit(solution)/shard_map/ppermute | solution.py:58
  118.0 10.9 %collective-permute-start.16 = (bf16[64,2048]{1,0:T(8,128)(2,1)S(1)}, bf16[64,2048]{1,0:T(8,128)(2,1)}, u32[]{:S(2)}, u32[]{:S(2)}) collective-permute-start(bf16[64,2048]{1,0:T(8,128)(2,1)S(1)} %fusion.9), channel_id=1, source_target_pairs={{0,2},{1,3},{2,0},{3,1},{4,6},{5,7},{6,4},{7,5},{8,10},{9,11},{10,... | collective-permute-start | bytes 786440 | tf_op jit(solution)/shard_map/ppermute | solution.py:58
  118.1 14.0 %collective-permute-start.17 = (bf16[64,2048]{1,0:T(8,128)(2,1)S(1)}, bf16[64,2048]{1,0:T(8,128)(2,1)}, u32[]{:S(2)}, u32[]{:S(2)}) collective-permute-start(bf16[64,2048]{1,0:T(8,128)(2,1)S(1)} %fusion.9), channel_id=1, source_target_pairs={{0,1},{1,2},{2,3},{3,0},{4,5},{5,6},{6,7},{7,4},{8,9},{9,10},{10,1... | collective-permute-start | bytes 786440 | tf_op jit(solution)/shard_map/ppermute | solution.py:58
  146.7 15.1 %collective-permute-start.18 = (bf16[64,2048]{1,0:T(8,128)(2,1)S(1)}, bf16[64,2048]{1,0:T(8,128)(2,1)S(1)}, u32[]{:S(2)}, u32[]{:S(2)}) collective-permute-start(bf16[64,2048]{1,0:T(8,128)(2,1)S(1)} %get-tuple-element.131), channel_id=1, source_target_pairs={{0,1},{1,2},{2,3},{3,0},{4,5},{5,6},{6,7},{7,4},{8,9},{9,10},{10,1... | collective-permute-start | bytes 786440 | tf_op jit(solution)/shard_map/ppermute | solution.py:58
  146.8 15.0 %collective-permute-start.19 = (bf16[64,2048]{1,0:T(8,128)(2,1)S(1)}, bf16[64,2048]{1,0:T(8,128)(2,1)S(1)}, u32[]{:S(2)}, u32[]{:S(2)}) collective-permute-start(bf16[64,2048]{1,0:T(8,128)(2,1)S(1)} %get-tuple-element.133), channel_id=1, source_target_pairs={{0,3},{1,0},{2,1},{3,2},{4,7},{5,4},{6,5},{7,6},{8,11},{9,8},{10,9... | collective-permute-start | bytes 786440 | tf_op jit(solution)/shard_map/ppermute | solution.py:58
  150.0 11.8 %collective-permute-start.20 = (bf16[64,2048]{1,0:T(8,128)(2,1)S(1)}, bf16[64,2048]{1,0:T(8,128)(2,1)S(1)}, u32[]{:S(2)}, u32[]{:S(2)}) collective-permute-start(bf16[64,2048]{1,0:T(8,128)(2,1)S(1)} %get-tuple-element.132), channel_id=1, source_target_pairs={{0,2},{1,3},{2,0},{3,1},{4,6},{5,7},{6,4},{7,5},{8,10},{9,11},{10,... | collective-permute-start | bytes 786440 | tf_op jit(solution)/shard_map/ppermute | solution.py:58
  150.1 96.1 %collective-permute-start.72 = (bf16[256,512]{1,0:T(8,128)(2,1)S(1)}, bf16[256,512]{1,0:T(8,128)(2,1)S(1)}, u32[]{:S(2)}, u32[]{:S(2)}) collective-permute-start(bf16[256,512]{1,0:T(8,128)(2,1)S(1)} %pad_maximum_fusion.10.b0), channel_id=1, source_target_pairs={{0,4},{4,0},{1,5},{5,1},{2,6},{6,2},{3,7},{7,3},{8,12},{12,8},{9,1... | collective-permute-start | bytes 786440 | tf_op jit(solution)/shard_map/ppermute | solution.py:49
  153.3 126.2 %collective-permute-start.73 = (bf16[1024,256]{1,0:T(8,128)(2,1)}, bf16[1024,256]{1,0:T(8,128)(2,1)}, u32[]{:S(2)}, u32[]{:S(2)}) collective-permute-start(bf16[1024,256]{1,0:T(8,128)(2,1)} %get-tuple-element.81), channel_id=1, source_target_pairs={{0,4},{4,0},{1,5},{5,1},{2,6},{6,2},{3,7},{7,3},{8,12},{12,8},{9,1... | collective-permute-start | bytes 1572872 | tf_op jit(solution)/shard_map/ppermute | solution.py:49
  162.7 14.0 %collective-permute-start.24 = (bf16[64,2048]{1,0:T(8,128)(2,1)S(1)}, bf16[64,2048]{1,0:T(8,128)(2,1)S(1)}, u32[]{:S(2)}, u32[]{:S(2)}) collective-permute-start(bf16[64,2048]{1,0:T(8,128)(2,1)S(1)} %multiply_convert_fusion.4), channel_id=1, source_target_pairs={{0,3},{1,0},{2,1},{3,2},{4,7},{5,4},{6,5},{7,6},{8,11},{9,8},{10,9... | collective-permute-start | bytes 786440 | tf_op jit(solution)/shard_map/ppermute | solution.py:58
  165.7 14.9 %collective-permute-start.25 = (bf16[64,2048]{1,0:T(8,128)(2,1)S(1)}, bf16[64,2048]{1,0:T(8,128)(2,1)S(1)}, u32[]{:S(2)}, u32[]{:S(2)}) collective-permute-start(bf16[64,2048]{1,0:T(8,128)(2,1)S(1)} %multiply_convert_fusion.4), channel_id=1, source_target_pairs={{0,2},{1,3},{2,0},{3,1},{4,6},{5,7},{6,4},{7,5},{8,10},{9,11},{10,... | collective-permute-start | bytes 786440 | tf_op jit(solution)/shard_map/ppermute | solution.py:58
  165.7 15.7 %collective-permute-start.26 = (bf16[64,2048]{1,0:T(8,128)(2,1)S(1)}, bf16[64,2048]{1,0:T(8,128)(2,1)S(1)}, u32[]{:S(2)}, u32[]{:S(2)}) collective-permute-start(bf16[64,2048]{1,0:T(8,128)(2,1)S(1)} %multiply_convert_fusion.4), channel_id=1, source_target_pairs={{0,1},{1,2},{2,3},{3,0},{4,5},{5,6},{6,7},{7,4},{8,9},{9,10},{10,1... | collective-permute-start | bytes 786440 | tf_op jit(solution)/shard_map/ppermute | solution.py:58
  176.7 25.0 %collective-permute-start.21 = (bf16[64,2048]{1,0:T(8,128)(2,1)S(1)}, bf16[64,2048]{1,0:T(8,128)(2,1)S(1)}, u32[]{:S(2)}, u32[]{:S(2)}) collective-permute-start(bf16[64,2048]{1,0:T(8,128)(2,1)S(1)} %get-tuple-element.103), channel_id=1, source_target_pairs={{0,3},{1,0},{2,1},{3,2},{4,7},{5,4},{6,5},{7,6},{8,11},{9,8},{10,9... | collective-permute-start | bytes 786440 | tf_op jit(solution)/shard_map/ppermute | solution.py:58
  180.6 23.7 %collective-permute-start.22 = (bf16[64,2048]{1,0:T(8,128)(2,1)S(1)}, bf16[64,2048]{1,0:T(8,128)(2,1)S(1)}, u32[]{:S(2)}, u32[]{:S(2)}) collective-permute-start(bf16[64,2048]{1,0:T(8,128)(2,1)S(1)} %get-tuple-element.103), channel_id=1, source_target_pairs={{0,2},{1,3},{2,0},{3,1},{4,6},{5,7},{6,4},{7,5},{8,10},{9,11},{10,... | collective-permute-start | bytes 786440 | tf_op jit(solution)/shard_map/ppermute | solution.py:58
  181.4 23.7 %collective-permute-start.23 = (bf16[64,2048]{1,0:T(8,128)(2,1)S(1)}, bf16[64,2048]{1,0:T(8,128)(2,1)S(1)}, u32[]{:S(2)}, u32[]{:S(2)}) collective-permute-start(bf16[64,2048]{1,0:T(8,128)(2,1)S(1)} %get-tuple-element.103), channel_id=1, source_target_pairs={{0,1},{1,2},{2,3},{3,0},{4,5},{5,6},{6,7},{7,4},{8,9},{9,10},{10,1... | collective-permute-start | bytes 786440 | tf_op jit(solution)/shard_map/ppermute | solution.py:58
  201.7 9.5 %collective-permute-start.27 = (bf16[64,2048]{1,0:T(8,128)(2,1)S(1)}, bf16[64,2048]{1,0:T(8,128)(2,1)S(1)}, u32[]{:S(2)}, u32[]{:S(2)}) collective-permute-start(bf16[64,2048]{1,0:T(8,128)(2,1)S(1)} %get-tuple-element.128), channel_id=1, source_target_pairs={{0,1},{1,2},{2,3},{3,0},{4,5},{5,6},{6,7},{7,4},{8,9},{9,10},{10,1... | collective-permute-start | bytes 786440 | tf_op jit(solution)/shard_map/ppermute | solution.py:58
  204.3 11.0 %collective-permute-start.28 = (bf16[64,2048]{1,0:T(8,128)(2,1)S(1)}, bf16[64,2048]{1,0:T(8,128)(2,1)S(1)}, u32[]{:S(2)}, u32[]{:S(2)}) collective-permute-start(bf16[64,2048]{1,0:T(8,128)(2,1)S(1)} %get-tuple-element.130), channel_id=1, source_target_pairs={{0,3},{1,0},{2,1},{3,2},{4,7},{5,4},{6,5},{7,6},{8,11},{9,8},{10,9... | collective-permute-start | bytes 786440 | tf_op jit(solution)/shard_map/ppermute | solution.py:58
  205.1 11.9 %collective-permute-start.29 = (bf16[64,2048]{1,0:T(8,128)(2,1)S(1)}, bf16[64,2048]{1,0:T(8,128)(2,1)S(1)}, u32[]{:S(2)}, u32[]{:S(2)}) collective-permute-start(bf16[64,2048]{1,0:T(8,128)(2,1)S(1)} %get-tuple-element.129), channel_id=1, source_target_pairs={{0,2},{1,3},{2,0},{3,1},{4,6},{5,7},{6,4},{7,5},{8,10},{9,11},{10,... | collective-permute-start | bytes 786440 | tf_op jit(solution)/shard_map/ppermute | solution.py:58
  227.7 9.3 %collective-permute-start.32 = (bf16[64,2048]{1,0:T(8,128)(2,1)S(1)}, bf16[64,2048]{1,0:T(8,128)(2,1)S(1)}, u32[]{:S(2)}, u32[]{:S(2)}) collective-permute-start(bf16[64,2048]{1,0:T(8,128)(2,1)S(1)} %multiply_convert_fusion.3), channel_id=1, source_target_pairs={{0,1},{1,2},{2,3},{3,0},{4,5},{5,6},{6,7},{7,4},{8,9},{9,10},{10,1... | collective-permute-start | bytes 786440 | tf_op jit(solution)/shard_map/ppermute | solution.py:58
  232.0 49.4 %collective-permute-start.83 = (bf16[256,2048]{1,0:T(8,128)(2,1)}, bf16[256,2048]{1,0:T(8,128)(2,1)}, u32[]{:S(2)}, u32[]{:S(2)}) collective-permute-start(bf16[256,2048]{1,0:T(8,128)(2,1)} %get-tuple-element.108.b0), channel_id=1, source_target_pairs={{0,4},{4,0},{1,5},{5,1},{2,6},{6,2},{3,7},{7,3},{8,12},{12,8},{9,1... | collective-permute-start | bytes 3145736 | tf_op jit(solution)/shard_map/ppermute | solution.py:49
  238.1 8.1 %collective-permute-start.71 = (bf16[1024,256]{1,0:T(8,128)(2,1)S(1)}, bf16[1024,256]{1,0:T(8,128)(2,1)S(1)}, u32[]{:S(2)}, u32[]{:S(2)}) collective-permute-start(bf16[1024,256]{1,0:T(8,128)(2,1)S(1)} %get-tuple-element.79), channel_id=1, source_target_pairs={{0,4},{4,0},{1,5},{5,1},{2,6},{6,2},{3,7},{7,3},{8,12},{12,8},{9,1... | collective-permute-start | bytes 1572872 | tf_op jit(solution)/shard_map/ppermute | solution.py:49
  248.0 231.4 %reduce-scatter.5.cloned.1.call-start = ((), (), s32[]{:S(2)}) async-start(), calls=%async_computation.3 | async-start | bytes 4456448 | tf_op jit(solution)/shard_map/reduce_scatter | solution.py:453
  260.7 33.1 %collective-permute-start.93 = (bf16[256,2048]{1,0:T(8,128)(2,1)S(1)}, bf16[256,2048]{1,0:T(8,128)(2,1)S(1)}, u32[]{:S(2)}, u32[]{:S(2)}) collective-permute-start(bf16[256,2048]{1,0:T(8,128)(2,1)S(1)} %copy-done.41), channel_id=1, source_target_pairs={{0,4},{4,0},{1,5},{5,1},{2,6},{6,2},{3,7},{7,3},{8,12},{12,8},{9,1... | collective-permute-start | bytes 3145736 | tf_op jit(solution)/shard_map/ppermute | solution.py:49
  260.8 37.4 %collective-permute-start.74 = (bf16[256,2048]{1,0:T(8,128)(2,1)}, bf16[256,2048]{1,0:T(8,128)(2,1)}, u32[]{:S(2)}, u32[]{:S(2)}) collective-permute-start(bf16[256,2048]{1,0:T(8,128)(2,1)} %get-tuple-element.109.b0), channel_id=1, source_target_pairs={{0,4},{4,0},{1,5},{5,1},{2,6},{6,2},{3,7},{7,3},{8,12},{12,8},{9,1... | collective-permute-start | bytes 3145736 | tf_op jit(solution)/shard_map/ppermute | solution.py:49
  263.6 28.6 %collective-permute-start.92 = (bf16[1024,256]{1,0:T(8,128)(2,1)S(1)}, bf16[1024,256]{1,0:T(8,128)(2,1)S(1)}, u32[]{:S(2)}, u32[]{:S(2)}) collective-permute-start(bf16[1024,256]{1,0:T(8,128)(2,1)S(1)} %get-tuple-element.91), channel_id=1, source_target_pairs={{0,4},{4,0},{1,5},{5,1},{2,6},{6,2},{3,7},{7,3},{8,12},{12,8},{9,1... | collective-permute-start | bytes 1572872 | tf_op jit(solution)/shard_map/ppermute | solution.py:49
  279.6 27.7 %collective-permute-start.39 = (bf16[2,2,4,256,128]{4,3,1,2,0:T(8,128)(2,1)}, bf16[2,2,4,256,128]{4,3,1,2,0:T(8,128)(2,1)}, u32[]{:S(2)}, u32[]{:S(2)}) collective-permute-start(bf16[2,2,4,256,128]{4,3,1,2,0:T(8,128)(2,1)} %copy.142), channel_id=1, source_target_pairs={{0,4},{4,0},{1,5},{5,1},{2,6},{6,2},{3,7},{7,3},{8,12},{12,8},{9,1... | collective-permute-start | bytes 3145736 | tf_op jit(solution)/shard_map/ppermute | solution.py:49
  286.0 27.2 %collective-permute-start.84 = (bf16[512,1024]{1,0:T(8,128)(2,1)}, bf16[512,1024]{1,0:T(8,128)(2,1)}, u32[]{:S(2)}, u32[]{:S(2)}) collective-permute-start(bf16[512,1024]{1,0:T(8,128)(2,1)} %get-tuple-element.87), channel_id=1, source_target_pairs={{0,8},{8,0},{16,24},{24,16},{1,9},{9,1},{17,25},{25,17},{2,10},{10... | collective-permute-start | bytes 3145736 | tf_op jit(solution)/shard_map/ppermute | solution.py:45
  292.2 28.6 %collective-permute-start.88 = (bf16[512,1024]{1,0:T(8,128)(2,1)}, bf16[512,1024]{1,0:T(8,128)(2,1)}, u32[]{:S(2)}, u32[]{:S(2)}) collective-permute-start(bf16[512,1024]{1,0:T(8,128)(2,1)} %get-tuple-element.89), channel_id=1, source_target_pairs={{0,24},{8,16},{16,8},{24,0},{1,25},{9,17},{17,9},{25,1},{2,26},{10... | collective-permute-start | bytes 3145736 | tf_op jit(solution)/shard_map/ppermute | solution.py:45
  302.0 26.7 %collective-permute-start.75 = (bf16[512,1024]{1,0:T(8,128)(2,1)S(1)}, bf16[512,1024]{1,0:T(8,128)(2,1)S(1)}, u32[]{:S(2)}, u32[]{:S(2)}) collective-permute-start(bf16[512,1024]{1,0:T(8,128)(2,1)S(1)} %get-tuple-element.83), channel_id=1, source_target_pairs={{0,32},{32,0},{64,96},{96,64},{1,33},{33,1},{65,97},{97,65},{2,34}... | collective-permute-start | bytes 3145736 | tf_op jit(solution)/shard_map/ppermute | solution.py:45
  303.2 33.0 %collective-permute-start.36 = (bf16[256,128]{1,0:T(8,128)(2,1)S(1)}, bf16[256,128]{1,0:T(8,128)(2,1)S(1)}, u32[]{:S(2)}, u32[]{:S(2)}) collective-permute-start(bf16[256,128]{1,0:T(8,128)(2,1)S(1)} %get-tuple-element.158), channel_id=1, source_target_pairs={{0,24},{8,16},{16,8},{24,0},{1,25},{9,17},{17,9},{25,1},{2,26},{10... | collective-permute-start | bytes 196616 | tf_op jit(solution)/shard_map/ppermute | solution.py:45
  307.3 36.9 %collective-permute-start.37 = (bf16[256,128]{1,0:T(8,128)(2,1)S(1)}, bf16[256,128]{1,0:T(8,128)(2,1)S(1)}, u32[]{:S(2)}, u32[]{:S(2)}) collective-permute-start(bf16[256,128]{1,0:T(8,128)(2,1)S(1)} %get-tuple-element.157), channel_id=1, source_target_pairs={{0,32},{32,0},{64,96},{96,64},{1,33},{33,1},{65,97},{97,65},{2,34}... | collective-permute-start | bytes 196616 | tf_op jit(solution)/shard_map/ppermute | solution.py:45
  313.2 28.8 %collective-permute-start.79 = (bf16[512,1024]{1,0:T(8,128)(2,1)S(1)}, bf16[512,1024]{1,0:T(8,128)(2,1)S(1)}, u32[]{:S(2)}, u32[]{:S(2)}) collective-permute-start(bf16[512,1024]{1,0:T(8,128)(2,1)S(1)} %get-tuple-element.85), channel_id=1, source_target_pairs={{0,96},{32,64},{64,32},{96,0},{1,97},{33,65},{65,33},{97,1},{2,98}... | collective-permute-start | bytes 3145736 | tf_op jit(solution)/shard_map/ppermute | solution.py:45
  320.8 12.3 %collective-permute-start.40 = (bf16[2,4,256,128]{3,2,0,1:T(8,128)(2,1)S(1)}, bf16[2,4,256,128]{3,2,0,1:T(8,128)(2,1)S(1)}, u32[]{:S(2)}, u32[]{:S(2)}) collective-permute-start(bf16[2,4,256,128]{3,2,0,1:T(8,128)(2,1)S(1)} %fusion.4), channel_id=1, source_target_pairs={{0,8},{8,0},{16,24},{24,16},{1,9},{9,1},{17,25},{25,17},{2,10},{10... | collective-permute-start | bytes 1572872 | tf_op jit(solution)/shard_map/ppermute | solution.py:45
  328.7 15.5 %collective-permute-start.38 = (bf16[256,128]{1,0:T(8,128)(2,1)S(1)}, bf16[256,128]{1,0:T(8,128)(2,1)S(1)}, u32[]{:S(2)}, u32[]{:S(2)}) collective-permute-start(bf16[256,128]{1,0:T(8,128)(2,1)S(1)} %get-tuple-element.156), channel_id=1, source_target_pairs={{0,56},{8,48},{16,40},{24,32},{32,24},{40,16},{48,8},{56,0},{64,12... | collective-permute-start | bytes 196616 | tf_op jit(solution)/shard_map/ppermute | solution.py:54
  334.5 9.7 %collective-permute-start.41 = (bf16[2,256,128]{2,1,0:T(8,128)(2,1)S(1)}, bf16[2,256,128]{2,1,0:T(8,128)(2,1)S(1)}, u32[]{:S(2)}, u32[]{:S(2)}) collective-permute-start(bf16[2,256,128]{2,1,0:T(8,128)(2,1)S(1)} %get-tuple-element.145), channel_id=1, source_target_pairs={{0,24},{8,16},{16,8},{24,0},{1,25},{9,17},{17,9},{25,1},{2,26},{10... | collective-permute-start | bytes 393224 | tf_op jit(solution)/shard_map/ppermute | solution.py:45
  344.2 93.7 %collective-permute-start.53 = (bf16[1024,256]{1,0:T(8,128)(2,1)}, bf16[1024,256]{1,0:T(8,128)(2,1)S(1)}, u32[]{:S(2)}, u32[]{:S(2)}) collective-permute-start(bf16[1024,256]{1,0:T(8,128)(2,1)} %get-tuple-element.69), channel_id=1, source_target_pairs={{0,4},{4,0},{1,5},{5,1},{2,6},{6,2},{3,7},{7,3},{8,12},{12,8},{9,1... | collective-permute-start | bytes 1572872 | tf_op jit(solution)/shard_map/ppermute | solution.py:49
  376.5 9.5 %collective-permute-start.47 = (bf16[64,2048]{1,0:T(8,128)(2,1)S(1)}, bf16[64,2048]{1,0:T(8,128)(2,1)S(1)}, u32[]{:S(2)}, u32[]{:S(2)}) collective-permute-start(bf16[64,2048]{1,0:T(8,128)(2,1)S(1)} %get-tuple-element.125), channel_id=1, source_target_pairs={{0,1},{1,2},{2,3},{3,0},{4,5},{5,6},{6,7},{7,4},{8,9},{9,10},{10,1... | collective-permute-start | bytes 786440 | tf_op jit(solution)/shard_map/ppermute | solution.py:58
  378.1 8.5 %collective-permute-start.48 = (bf16[64,2048]{1,0:T(8,128)(2,1)S(1)}, bf16[64,2048]{1,0:T(8,128)(2,1)S(1)}, u32[]{:S(2)}, u32[]{:S(2)}) collective-permute-start(bf16[64,2048]{1,0:T(8,128)(2,1)S(1)} %get-tuple-element.127), channel_id=1, source_target_pairs={{0,3},{1,0},{2,1},{3,2},{4,7},{5,4},{6,5},{7,6},{8,11},{9,8},{10,9... | collective-permute-start | bytes 786440 | tf_op jit(solution)/shard_map/ppermute | solution.py:58
  379.9 8.5 %collective-permute-start.49 = (bf16[64,2048]{1,0:T(8,128)(2,1)S(1)}, bf16[64,2048]{1,0:T(8,128)(2,1)S(1)}, u32[]{:S(2)}, u32[]{:S(2)}) collective-permute-start(bf16[64,2048]{1,0:T(8,128)(2,1)S(1)} %get-tuple-element.126), channel_id=1, source_target_pairs={{0,2},{1,3},{2,0},{3,1},{4,6},{5,7},{6,4},{7,5},{8,10},{9,11},{10,... | collective-permute-start | bytes 786440 | tf_op jit(solution)/shard_map/ppermute | solution.py:58
  383.2 19.4 %collective-permute-start.85 = (bf16[256,1024]{1,0:T(8,128)(2,1)S(1)}, bf16[256,1024]{1,0:T(8,128)(2,1)S(1)}, u32[]{:S(2)}, u32[]{:S(2)}) collective-permute-start(bf16[256,1024]{1,0:T(8,128)(2,1)S(1)} %bitcast.364), channel_id=1, source_target_pairs={{0,24},{8,16},{16,8},{24,0},{1,25},{9,17},{17,9},{25,1},{2,26},{10... | collective-permute-start | bytes 1572872 | tf_op jit(solution)/shard_map/ppermute | solution.py:45
  385.9 19.0 %collective-permute-start.89 = (bf16[256,1024]{1,0:T(8,128)(2,1)S(1)}, bf16[256,1024]{1,0:T(8,128)(2,1)S(1)}, u32[]{:S(2)}, u32[]{:S(2)}) collective-permute-start(bf16[256,1024]{1,0:T(8,128)(2,1)S(1)} %bitcast.362), channel_id=1, source_target_pairs={{0,32},{32,0},{64,96},{96,64},{1,33},{33,1},{65,97},{97,65},{2,34}... | collective-permute-start | bytes 1572872 | tf_op jit(solution)/shard_map/ppermute | solution.py:45
  386.6 20.7 %collective-permute-start.76 = (bf16[256,1024]{1,0:T(8,128)(2,1)S(1)}, bf16[256,1024]{1,0:T(8,128)(2,1)S(1)}, u32[]{:S(2)}, u32[]{:S(2)}) collective-permute-start(bf16[256,1024]{1,0:T(8,128)(2,1)S(1)} %bitcast.363), channel_id=1, source_target_pairs={{0,96},{32,64},{64,32},{96,0},{1,97},{33,65},{65,33},{97,1},{2,98}... | collective-permute-start | bytes 1572872 | tf_op jit(solution)/shard_map/ppermute | solution.py:45
  388.4 15.6 %collective-permute-start.80 = (bf16[256,1024]{1,0:T(8,128)(2,1)S(1)}, bf16[256,1024]{1,0:T(8,128)(2,1)S(1)}, u32[]{:S(2)}, u32[]{:S(2)}) collective-permute-start(bf16[256,1024]{1,0:T(8,128)(2,1)S(1)} %bitcast.357), channel_id=1, source_target_pairs={{0,8},{8,0},{16,24},{24,16},{1,9},{9,1},{17,25},{25,17},{2,10},{10... | collective-permute-start | bytes 1572872 | tf_op jit(solution)/shard_map/ppermute | solution.py:45
  402.6 35.3 %collective-permute-start.54 = (bf16[256,1536]{1,0:T(8,128)(2,1)S(1)}, bf16[256,1536]{1,0:T(8,128)(2,1)S(1)}, u32[]{:S(2)}, u32[]{:S(2)}) collective-permute-start(bf16[256,1536]{1,0:T(8,128)(2,1)S(1)} %pad_maximum_fusion.3.b0), channel_id=1, source_target_pairs={{0,4},{4,0},{1,5},{5,1},{2,6},{6,2},{3,7},{7,3},{8,12},{12,8},{9,1... | collective-permute-start | bytes 2359304 | tf_op jit(solution)/shard_map/ppermute | solution.py:49
  404.1 9.2 %collective-permute-start.50 = (bf16[64,2048]{1,0:T(8,128)(2,1)S(1)}, bf16[64,2048]{1,0:T(8,128)(2,1)S(1)}, u32[]{:S(2)}, u32[]{:S(2)}) collective-permute-start(bf16[64,2048]{1,0:T(8,128)(2,1)S(1)} %get-tuple-element.98), channel_id=1, source_target_pairs={{0,3},{1,0},{2,1},{3,2},{4,7},{5,4},{6,5},{7,6},{8,11},{9,8},{10,9... | collective-permute-start | bytes 786440 | tf_op jit(solution)/shard_map/ppermute | solution.py:58
  405.0 10.9 %collective-permute-start.51 = (bf16[64,2048]{1,0:T(8,128)(2,1)S(1)}, bf16[64,2048]{1,0:T(8,128)(2,1)S(1)}, u32[]{:S(2)}, u32[]{:S(2)}) collective-permute-start(bf16[64,2048]{1,0:T(8,128)(2,1)S(1)} %get-tuple-element.98), channel_id=1, source_target_pairs={{0,2},{1,3},{2,0},{3,1},{4,6},{5,7},{6,4},{7,5},{8,10},{9,11},{10,... | collective-permute-start | bytes 786440 | tf_op jit(solution)/shard_map/ppermute | solution.py:58
  407.4 12.3 %collective-permute-start.52 = (bf16[64,2048]{1,0:T(8,128)(2,1)S(1)}, bf16[64,2048]{1,0:T(8,128)(2,1)S(1)}, u32[]{:S(2)}, u32[]{:S(2)}) collective-permute-start(bf16[64,2048]{1,0:T(8,128)(2,1)S(1)} %get-tuple-element.98), channel_id=1, source_target_pairs={{0,1},{1,2},{2,3},{3,0},{4,5},{5,6},{6,7},{7,4},{8,9},{9,10},{10,1... | collective-permute-start | bytes 786440 | tf_op jit(solution)/shard_map/ppermute | solution.py:58
  419.7 8.2 %collective-permute-start.77 = (bf16[128,1024]{1,0:T(8,128)(2,1)S(1)}, bf16[128,1024]{1,0:T(8,128)(2,1)S(1)}, u32[]{:S(2)}, u32[]{:S(2)}) collective-permute-start(bf16[128,1024]{1,0:T(8,128)(2,1)S(1)} %bitcast.376), channel_id=1, source_target_pairs={{0,8},{8,0},{16,24},{24,16},{1,9},{9,1},{17,25},{25,17},{2,10},{10... | collective-permute-start | bytes 786440 | tf_op jit(solution)/shard_map/ppermute | solution.py:45
  421.4 9.4 %collective-permute-start.81 = (bf16[128,1024]{1,0:T(8,128)(2,1)S(1)}, bf16[128,1024]{1,0:T(8,128)(2,1)S(1)}, u32[]{:S(2)}, u32[]{:S(2)}) collective-permute-start(bf16[128,1024]{1,0:T(8,128)(2,1)S(1)} %bitcast.365), channel_id=1, source_target_pairs={{0,24},{8,16},{16,8},{24,0},{1,25},{9,17},{17,9},{25,1},{2,26},{10... | collective-permute-start | bytes 786440 | tf_op jit(solution)/shard_map/ppermute | solution.py:45
  423.4 9.0 %collective-permute-start.87 = (bf16[64,1024]{1,0:T(8,128)(2,1)S(1)}, bf16[64,1024]{1,0:T(8,128)(2,1)S(1)}, u32[]{:S(2)}, u32[]{:S(2)}) collective-permute-start(bf16[64,1024]{1,0:T(8,128)(2,1)S(1)} %fusion.19), channel_id=1, source_target_pairs={{0,96},{32,64},{64,32},{96,0},{1,97},{33,65},{65,33},{97,1},{2,98}... | collective-permute-start | bytes 393224 | tf_op jit(solution)/shard_map/ppermute | solution.py:45
  440.2 13.2 %collective-permute-start.55 = (bf16[512,384]{1,0:T(8,128)(2,1)}, bf16[512,384]{1,0:T(8,128)(2,1)}, u32[]{:S(2)}, u32[]{:S(2)}) collective-permute-start(bf16[512,384]{1,0:T(8,128)(2,1)} %get-tuple-element.71), channel_id=1, source_target_pairs={{0,32},{32,0},{64,96},{96,64},{1,33},{33,1},{65,97},{97,65},{2,34}... | collective-permute-start | bytes 1179656 | tf_op jit(solution)/shard_map/ppermute | solution.py:45
  443.7 12.1 %collective-permute-start.59 = (bf16[512,384]{1,0:T(8,128)(2,1)}, bf16[512,384]{1,0:T(8,128)(2,1)}, u32[]{:S(2)}, u32[]{:S(2)}) collective-permute-start(bf16[512,384]{1,0:T(8,128)(2,1)} %get-tuple-element.73), channel_id=1, source_target_pairs={{0,96},{32,64},{64,32},{96,0},{1,97},{33,65},{65,33},{97,1},{2,98}... | collective-permute-start | bytes 1179656 | tf_op jit(solution)/shard_map/ppermute | solution.py:45
  448.4 10.0 %collective-permute-start.63 = (bf16[512,384]{1,0:T(8,128)(2,1)}, bf16[512,384]{1,0:T(8,128)(2,1)}, u32[]{:S(2)}, u32[]{:S(2)}) collective-permute-start(bf16[512,384]{1,0:T(8,128)(2,1)} %get-tuple-element.75), channel_id=1, source_target_pairs={{0,8},{8,0},{16,24},{24,16},{1,9},{9,1},{17,25},{25,17},{2,10},{10... | collective-permute-start | bytes 1179656 | tf_op jit(solution)/shard_map/ppermute | solution.py:45
  450.6 11.0 %collective-permute-start.67 = (bf16[512,384]{1,0:T(8,128)(2,1)}, bf16[512,384]{1,0:T(8,128)(2,1)}, u32[]{:S(2)}, u32[]{:S(2)}) collective-permute-start(bf16[512,384]{1,0:T(8,128)(2,1)} %get-tuple-element.77), channel_id=1, source_target_pairs={{0,24},{8,16},{16,8},{24,0},{1,25},{9,17},{17,9},{25,1},{2,26},{10... | collective-permute-start | bytes 1179656 | tf_op jit(solution)/shard_map/ppermute | solution.py:45
  454.8 9.3 %collective-permute-start.56 = (bf16[256,384]{1,0:T(8,128)(2,1)S(1)}, bf16[256,384]{1,0:T(8,128)(2,1)S(1)}, u32[]{:S(2)}, u32[]{:S(2)}) collective-permute-start(bf16[256,384]{1,0:T(8,128)(2,1)S(1)} %bitcast.379), channel_id=1, source_target_pairs={{0,96},{32,64},{64,32},{96,0},{1,97},{33,65},{65,33},{97,1},{2,98}... | collective-permute-start | bytes 589832 | tf_op jit(solution)/shard_map/ppermute | solution.py:45
  (153 other events, 1327.0 us)
Sparse Core Ops, SparseCore 0:
  248.1 71.6 reduce-scatter.2
  323.5 79.7 reduce-scatter.4
